TPU v7x, 32 devices: a whole 2x2x4 slice. The times are simulated.
32 devices in a mesh: seq: 16 (over z, y, core), head: 2 (over x).
Axes of the slice: x: 2, y: 2, z: 4, core: 2. Of those that a mesh axis runs over, the one named last changes fastest.
Arguments:
- query_rows: bfloat16 [4096, 3072], P(('seq', 'head')), may hold values from -16 to 16
- key_rows: bfloat16 [4096, 1024], P(('seq', 'head')), may hold values from -16 to 16
- value_rows: bfloat16 [4096, 1024], P(('seq', 'head')), may hold values from -6 to 6
- residual: bfloat16 [4096, 3072], P(('seq', 'head')), may hold values from -6 to 6
- out_weight: bfloat16 [3072, 3072], P('head'), may hold values from -0.109375 to 0.109375
- gate_table: float32 [64, 3072], replicated, may hold values from -4 to 4
- noise_steps: int32 [8], replicated, may hold values from 0 to 63
- segment_mask: int32 [8, 8], replicated, may hold values from 0 to 1, as said below
- segment_map: int32 [16], replicated, may hold values from 0 to 7, as said below
Outputs:
- layer_output: bfloat16 [4096, 3072], P(('seq', 'head'))
Inputs may be any that keep to these rules, and one draw needn't show every extreme that they name: `segment_mask`: ones on the diagonal, zeros above it. `segment_map`: each segment number stands in exactly 2 entries.
All inputs are finite; a program needn't handle non-finite values.
Results may differ from a plain program's by a relative error of at most 0.0095.
Values may be sent and summed in bfloat16 or wider, within the bound.
No kernel may reach another device: no remote copies, remote signals or barrier semaphores. Data moves between devices by JAX's collectives and lax.ppermute only.
A program may use at most 64 MiB of HBM per device.

v0:
```python
import math

import jax
import jax.numpy as jnp
from jax import lax
from jax.sharding import PartitionSpec as P

Q_HEADS = 24
KV_HEADS = 8
HEAD_DIM = 128


NEG = -1e30


def lookup(source_table, position):
    matches = jnp.arange(source_table.shape[0], dtype=jnp.int32) == position
    shaped = matches.reshape((-1,) + (1,) * (source_table.ndim - 1))
    return jnp.sum(jnp.where(shaped, source_table, jnp.zeros_like(source_table)), axis=0)


def visible_keys(owners, segment_map, mask_row):
    places = jnp.arange(segment_map.shape[0], dtype=jnp.int32)
    segment_ids = jnp.sum(
        jnp.where(owners[:, None] == places[None, :], segment_map[None, :], 0), axis=1
    )
    labels = jnp.arange(mask_row.shape[0], dtype=jnp.int32)
    return (
        jnp.sum(jnp.where(segment_ids[:, None] == labels[None, :], mask_row[None, :], 0), axis=1)
        > 0
    )


def attend_block(state_now, grouped, key_blk, value_blk, visible):
    running_max, weight_sum, accumulated = state_now
    kv_local = grouped.shape[1]
    head_size = grouped.shape[3]
    keys_three = key_blk.reshape(key_blk.shape[0], kv_local, head_size)
    values_three = value_blk.reshape(value_blk.shape[0], kv_local, head_size)
    scores = jnp.einsum(
        "qcgd,kcd->cgqk", grouped, keys_three, preferred_element_type=jnp.float32
    ) * head_size ** (-0.5)
    scores = jnp.where(visible, scores, NEG)
    new_max = jnp.maximum(running_max, jnp.max(scores, axis=-1))
    weights = jnp.where(visible, jnp.exp(scores - new_max[..., None]), 0.0)
    factor = jnp.exp(running_max - new_max)
    weight_sum = weight_sum * factor + jnp.sum(weights, axis=-1)
    product = jnp.einsum(
        "cgqk,kcd->cgqd",
        weights.astype(jnp.bfloat16),
        values_three,
        preferred_element_type=jnp.float32,
    )
    accumulated = accumulated * factor[..., None] + product
    return (new_max, weight_sum, accumulated)


def sweep(state_now, grouped, key_part, value_part, visible, block_size):
    num_blocks = key_part.shape[0] // block_size
    stacked = (
        key_part.reshape(num_blocks, block_size, key_part.shape[1]),
        value_part.reshape(num_blocks, block_size, value_part.shape[1]),
        visible.reshape(num_blocks, block_size),
    )

    def scan_step(state_in, block_item):
        key_blk, value_blk, seen_blk = block_item
        state_out = attend_block(state_in, grouped, key_blk, value_blk, seen_blk)
        return (state_out, None)

    return lax.scan(scan_step, state_now, stacked)[0]


def per_device(
    query_rows,
    key_rows,
    value_rows,
    residual,
    out_weight,
    gate_table,
    noise_steps,
    segment_mask,
    segment_map,
):
    n_head = lax.axis_size("head")
    row_count = query_rows.shape[0]
    tok_dev = row_count * n_head
    group_size = Q_HEADS // KV_HEADS
    kv_local = KV_HEADS // n_head
    local_queries = lax.all_to_all(query_rows, "head", split_axis=1, concat_axis=0, tiled=True)
    grouped = local_queries.reshape(tok_dev, kv_local, group_size, HEAD_DIM)
    own_segment = lookup(segment_map, lax.axis_index("seq"))
    mask_row = lookup(segment_mask, own_segment)
    initial = (
        jnp.full((kv_local, group_size, tok_dev), NEG, jnp.float32),
        jnp.zeros((kv_local, group_size, tok_dev), jnp.float32),
        jnp.zeros((kv_local, group_size, tok_dev, HEAD_DIM), jnp.float32),
    )
    local_keys, local_values = (
        lax.all_to_all(key_rows, "head", split_axis=1, concat_axis=0, tiled=True),
        lax.all_to_all(value_rows, "head", split_axis=1, concat_axis=0, tiled=True),
    )
    key_piece = lax.all_gather(local_keys, "seq", axis=0, tiled=True)
    value_piece = lax.all_gather(local_values, "seq", axis=0, tiled=True)
    piece_rows = key_piece.shape[0]
    owners = jnp.arange(piece_rows, dtype=jnp.int32) // tok_dev
    visible = visible_keys(owners, segment_map, mask_row)
    block_size = math.gcd(piece_rows, 512)
    final = sweep(initial, grouped, key_piece, value_piece, visible, block_size)
    running_max, weight_sum, accumulated = final
    normalized = accumulated / weight_sum[..., None]
    attended = jnp.transpose(normalized, (2, 0, 1, 3)).reshape(tok_dev, -1).astype(jnp.bfloat16)
    projected = lax.psum_scatter(
        jnp.dot(attended, out_weight, preferred_element_type=jnp.float32).astype(jnp.bfloat16),
        "head",
        scatter_dimension=0,
        tiled=True,
    ).astype(jnp.float32)
    step_now = lookup(noise_steps, own_segment)
    gate_row = lookup(gate_table, step_now)
    return (residual.astype(jnp.float32) + gate_row[None, :] * projected).astype(jnp.bfloat16)


def solution(mesh):
    placed = (
        P(("seq", "head"), None),
        P(("seq", "head"), None),
        P(("seq", "head"), None),
        P(("seq", "head"), None),
        P("head", None),
        P(),
        P(),
        P(),
        P(),
    )
    return jax.shard_map(
        per_device, mesh=mesh, in_specs=placed, out_specs=P(("seq", "head"), None), check_vma=False
    )
```

profile of v0, /device:TPU:0, one launch (start us, length us, event | category | flops | bytes accessed | tf_op | source)
XLA Modules:
  0.0 294.3 jit_solution(16626911149762772305)
XLA Ops:
  6.5 1.2 copy.55
  7.7 9.2 %all_to_all.54 = bf16[128,2,512]{0,2,1:T(8,128)(2,1)S(1)} all-to-all(bf16[128,2,512]{0,2,1:T(8,128)(2,1)S(1)} %bitcast.70), channel_id=1, replica_groups=mesh['seq'=16,'head'=2] {'head'}, dimensions={1} | all-to-all | bytes 524288 | tf_op jit(solution)/shard_map/all_to_all | solution.py:100
  16.9 0.8 copy.56
  17.8 1.1 copy.59
  19.0 7.6 %all_to_all.55 = bf16[128,2,512]{0,2,1:T(8,128)(2,1)S(1)} all-to-all(bf16[128,2,512]{0,2,1:T(8,128)(2,1)S(1)} %bitcast.71), channel_id=1, replica_groups=mesh['seq'=16,'head'=2] {'head'}, dimensions={1} | all-to-all | bytes 524288 | tf_op jit(solution)/shard_map/all_to_all | solution.py:101
  26.5 0.8 copy.60
  27.4 1.2 copy.57
  28.6 3.5 %all-to-all-start.1 = ((bf16[128,2,1536]{0,2,1:T(8,128)(2,1)}), bf16[128,2,1536]{0,2,1:T(8,128)(2,1)S(1)}, u32[]{:S(2)}, u32[]{:S(2)}) async-start(bf16[128,2,1536]{0,2,1:T(8,128)(2,1)} %bitcast.4), calls=%async_computation.1 | async-start | bytes 1572864 | tf_op jit(solution)/shard_map/all_to_all | solution.py:90
  32.2 0.6 fusion.18
  32.8 0.6 iota_compare_fusion.2
  33.8 6.7 %all-to-all-done.1 = bf16[128,2,1536]{0,2,1:T(8,128)(2,1)S(1)} async-done(((bf16[128,2,1536]{0,2,1:T(8,128)(2,1)}), bf16[128,2,1536]{0,2,1:T(8,128)(2,1)S(1)}, u32[]{:S(2)}, u32[]{:S(2)}) %all-to-all-start.1) | async-done | bytes 786464 | tf_op jit(solution)/shard_map/all_to_all | solution.py:90
  40.6 6.5 %copy.58 = bf16[2,128,1536]{1,0,2:T(2,128)(2,1)S(1)} copy(bf16[2,128,1536]{1,2,0:T(8,128)(2,1)S(1)} %bitcast.63) | data formatting | bytes 1572864 | tf_op jit(solution)/shard_map/all_to_all | solution.py:90
  47.1 0.5 reshape.64
  47.6 0.4 copy.62
  48.0 21.0 %all-gather.3.cloned.1.call-done = bf16[4096,512]{1,0:T(8,128)(2,1)} async-done(((bf16[256,512]{1,0:T(8,128)(2,1)}), bf16[4096,512]{1,0:T(8,128)(2,1)}) %all-gather.3.cloned.1.call-update) | async-done | bytes 4194320 | tf_op jit(solution)/shard_map/all_gather | solution.py:103
  68.9 51.2 %all-gather.5.cloned.1.call-done = bf16[4096,512]{1,0:T(8,128)(2,1)} async-done(((bf16[256,512]{1,0:T(8,128)(2,1)}), bf16[4096,512]{1,0:T(8,128)(2,1)}) %all-gather.5.cloned.1.call-update) | async-done | bytes 4194320 | tf_op jit(solution)/shard_map/all_gather | solution.py:104
  120.2 130.9 %while.15 = (s32[]{:T(128)}, f32[4,3,256]{2,1,0:T(4,128)S(1)}, f32[4,3,256]{2,1,0:T(4,128)S(1)}, f32[4,3,256,128]{3,2,1,0:T(8,128)}, pred[8,512]{1,0:T(8,128)(4,...) while((s32[]{:T(128)}, f32[4,3,256]{2,1,0:T(4,128)S(1)}, ...), condition=%wide.region_9.10_spmd.clone, body=%wide.region_6.9_spmd.clone.sunk | while | flops 826948608 | bytes 28248696 | solution.py:71
  120.2 1.3 constant_dynamic-slice_fusion.3
  121.7 4.2 %bitcast_reduce_fusion.2 = (f32[4,3,256]{2,1,0:T(4,128)S(1)}, f32[4,512,256,3]{2,1,3,0:T(8,128)}) fusion(pred[512]{0:T(512)(128)(4,1)S(1)} %dynamic-slice_reduce_fusion.2, bf16[512,4,128,1]{0,2,3,1:T(8,128)(2,1)S(1)} %bitcast.60, bf16[256,4,3,128]{3,0,2,1:T(8,128)(2,1)S(1)} %get-tuple-element.226), kind=kOutput, calls=%fused_computation.1.clone.1 | convolution fusion | flops 407368704 | bytes 7614976 | tf_op jit(solution)/shard_map/while/body/eval_jaxpr/qcgd,kcd->cgqk/dot_general | solution.py:40
  125.9 3.7 %fusion.35 = f32[4,3,256]{2,1,0:T(4,128)S(1)} fusion(f32[4,512,256,3]{2,1,3,0:T(8,128)} %get-tuple-element.196, f32[4,3,256]{2,1,0:T(4,128)S(1)} %select_maximum_fusion.2, pred[512]{0:T(512)(128)(4,1)S(1)} %dynamic-slice_reduce_fusion.2), kind=kLoop, calls=%fused_computation.6.clone.1 | loop fusion | flops 7861248 | bytes 6316544 | tf_op jit(solution)/shard_map/while/body/eval_jaxpr/reduce_sum | solution.py:47
  129.7 0.2 copy.77
  129.9 6.3 %fusion.37 = f32[4,3,256,128]{3,2,1,0:T(8,128)} fusion(f32[4,3,256,128]{3,2,1,0:T(8,128)} %get-tuple-element.213, bf16[512,4,128,1]{0,2,3,1:T(8,128)(2,1)S(1)} %bitcast.61, f32[4,512,256,3]{2,1,3,0:T(8,128)} %get-tuple-element.196, f32[4,3,256]{2,1,0:T(4,128)S(1)} %select_maximum_fusion.2, pred[512]{0:T(512)(128)(4,1)S(1)} %dynamic-slice_reduce_fusion.2, ...), kind=kOutput, calls=%fused_computation.11.clone.1 | convolution fusion | flops 411697152 | bytes 9986561 | tf_op jit(solution)/shard_map/while/body/eval_jaxpr/cgqk,kcd->cgqd/dot_general | solution.py:48
  136.2 1.3 constant_dynamic-slice_fusion.3
  137.4 0.2 copy.76
  137.7 4.2 %bitcast_reduce_fusion.2 = (f32[4,3,256]{2,1,0:T(4,128)S(1)}, f32[4,512,256,3]{2,1,3,0:T(8,128)}) fusion(pred[512]{0:T(512)(128)(4,1)S(1)} %dynamic-slice_reduce_fusion.2, bf16[512,4,128,1]{0,2,3,1:T(8,128)(2,1)S(1)} %bitcast.60, bf16[256,4,3,128]{3,0,2,1:T(8,128)(2,1)S(1)} %get-tuple-element.226), kind=kOutput, calls=%fused_computation.1.clone.1 | convolution fusion | flops 407368704 | bytes 7614976 | tf_op jit(solution)/shard_map/while/body/eval_jaxpr/qcgd,kcd->cgqk/dot_general | solution.py:40
  141.9 3.7 %fusion.35 = f32[4,3,256]{2,1,0:T(4,128)S(1)} fusion(f32[4,512,256,3]{2,1,3,0:T(8,128)} %get-tuple-element.196, f32[4,3,256]{2,1,0:T(4,128)S(1)} %select_maximum_fusion.2, pred[512]{0:T(512)(128)(4,1)S(1)} %dynamic-slice_reduce_fusion.2), kind=kLoop, calls=%fused_computation.6.clone.1 | loop fusion | flops 7861248 | bytes 6316544 | tf_op jit(solution)/shard_map/while/body/eval_jaxpr/reduce_sum | solution.py:47
  145.9 6.7 %fusion.37 = f32[4,3,256,128]{3,2,1,0:T(8,128)} fusion(f32[4,3,256,128]{3,2,1,0:T(8,128)} %get-tuple-element.213, bf16[512,4,128,1]{0,2,3,1:T(8,128)(2,1)S(1)} %bitcast.61, f32[4,512,256,3]{2,1,3,0:T(8,128)} %get-tuple-element.196, f32[4,3,256]{2,1,0:T(4,128)S(1)} %select_maximum_fusion.2, pred[512]{0:T(512)(128)(4,1)S(1)} %dynamic-slice_reduce_fusion.2, ...), kind=kOutput, calls=%fused_computation.11.clone.1 | convolution fusion | flops 411697152 | bytes 9986561 | tf_op jit(solution)/shard_map/while/body/eval_jaxpr/cgqk,kcd->cgqd/dot_general | solution.py:48
  152.6 1.3 constant_dynamic-slice_fusion.3
  153.9 0.2 copy.76
  154.1 4.2 %bitcast_reduce_fusion.2 = (f32[4,3,256]{2,1,0:T(4,128)S(1)}, f32[4,512,256,3]{2,1,3,0:T(8,128)}) fusion(pred[512]{0:T(512)(128)(4,1)S(1)} %dynamic-slice_reduce_fusion.2, bf16[512,4,128,1]{0,2,3,1:T(8,128)(2,1)S(1)} %bitcast.60, bf16[256,4,3,128]{3,0,2,1:T(8,128)(2,1)S(1)} %get-tuple-element.226), kind=kOutput, calls=%fused_computation.1.clone.1 | convolution fusion | flops 407368704 | bytes 7614976 | tf_op jit(solution)/shard_map/while/body/eval_jaxpr/qcgd,kcd->cgqk/dot_general | solution.py:40
  158.3 3.7 %fusion.35 = f32[4,3,256]{2,1,0:T(4,128)S(1)} fusion(f32[4,512,256,3]{2,1,3,0:T(8,128)} %get-tuple-element.196, f32[4,3,256]{2,1,0:T(4,128)S(1)} %select_maximum_fusion.2, pred[512]{0:T(512)(128)(4,1)S(1)} %dynamic-slice_reduce_fusion.2), kind=kLoop, calls=%fused_computation.6.clone.1 | loop fusion | flops 7861248 | bytes 6316544 | tf_op jit(solution)/shard_map/while/body/eval_jaxpr/reduce_sum | solution.py:47
  162.1 0.2 copy.77
  162.3 6.7 %fusion.37 = f32[4,3,256,128]{3,2,1,0:T(8,128)} fusion(f32[4,3,256,128]{3,2,1,0:T(8,128)} %get-tuple-element.213, bf16[512,4,128,1]{0,2,3,1:T(8,128)(2,1)S(1)} %bitcast.61, f32[4,512,256,3]{2,1,3,0:T(8,128)} %get-tuple-element.196, f32[4,3,256]{2,1,0:T(4,128)S(1)} %select_maximum_fusion.2, pred[512]{0:T(512)(128)(4,1)S(1)} %dynamic-slice_reduce_fusion.2, ...), kind=kOutput, calls=%fused_computation.11.clone.1 | convolution fusion | flops 411697152 | bytes 9986561 | tf_op jit(solution)/shard_map/while/body/eval_jaxpr/cgqk,kcd->cgqd/dot_general | solution.py:48
  169.0 1.3 constant_dynamic-slice_fusion.3
  170.3 0.2 copy.76
  170.5 4.2 %bitcast_reduce_fusion.2 = (f32[4,3,256]{2,1,0:T(4,128)S(1)}, f32[4,512,256,3]{2,1,3,0:T(8,128)}) fusion(pred[512]{0:T(512)(128)(4,1)S(1)} %dynamic-slice_reduce_fusion.2, bf16[512,4,128,1]{0,2,3,1:T(8,128)(2,1)S(1)} %bitcast.60, bf16[256,4,3,128]{3,0,2,1:T(8,128)(2,1)S(1)} %get-tuple-element.226), kind=kOutput, calls=%fused_computation.1.clone.1 | convolution fusion | flops 407368704 | bytes 7614976 | tf_op jit(solution)/shard_map/while/body/eval_jaxpr/qcgd,kcd->cgqk/dot_general | solution.py:40
  174.7 3.7 %fusion.35 = f32[4,3,256]{2,1,0:T(4,128)S(1)} fusion(f32[4,512,256,3]{2,1,3,0:T(8,128)} %get-tuple-element.196, f32[4,3,256]{2,1,0:T(4,128)S(1)} %select_maximum_fusion.2, pred[512]{0:T(512)(128)(4,1)S(1)} %dynamic-slice_reduce_fusion.2), kind=kLoop, calls=%fused_computation.6.clone.1 | loop fusion | flops 7861248 | bytes 6316544 | tf_op jit(solution)/shard_map/while/body/eval_jaxpr/reduce_sum | solution.py:47
  178.5 0.2 copy.77
  178.7 6.7 %fusion.37 = f32[4,3,256,128]{3,2,1,0:T(8,128)} fusion(f32[4,3,256,128]{3,2,1,0:T(8,128)} %get-tuple-element.213, bf16[512,4,128,1]{0,2,3,1:T(8,128)(2,1)S(1)} %bitcast.61, f32[4,512,256,3]{2,1,3,0:T(8,128)} %get-tuple-element.196, f32[4,3,256]{2,1,0:T(4,128)S(1)} %select_maximum_fusion.2, pred[512]{0:T(512)(128)(4,1)S(1)} %dynamic-slice_reduce_fusion.2, ...), kind=kOutput, calls=%fused_computation.11.clone.1 | convolution fusion | flops 411697152 | bytes 9986561 | tf_op jit(solution)/shard_map/while/body/eval_jaxpr/cgqk,kcd->cgqd/dot_general | solution.py:48
  185.4 1.3 constant_dynamic-slice_fusion.3
  186.7 0.2 copy.76
  187.0 4.2 %bitcast_reduce_fusion.2 = (f32[4,3,256]{2,1,0:T(4,128)S(1)}, f32[4,512,256,3]{2,1,3,0:T(8,128)}) fusion(pred[512]{0:T(512)(128)(4,1)S(1)} %dynamic-slice_reduce_fusion.2, bf16[512,4,128,1]{0,2,3,1:T(8,128)(2,1)S(1)} %bitcast.60, bf16[256,4,3,128]{3,0,2,1:T(8,128)(2,1)S(1)} %get-tuple-element.226), kind=kOutput, calls=%fused_computation.1.clone.1 | convolution fusion | flops 407368704 | bytes 7614976 | tf_op jit(solution)/shard_map/while/body/eval_jaxpr/qcgd,kcd->cgqk/dot_general | solution.py:40
  191.1 3.7 %fusion.35 = f32[4,3,256]{2,1,0:T(4,128)S(1)} fusion(f32[4,512,256,3]{2,1,3,0:T(8,128)} %get-tuple-element.196, f32[4,3,256]{2,1,0:T(4,128)S(1)} %select_maximum_fusion.2, pred[512]{0:T(512)(128)(4,1)S(1)} %dynamic-slice_reduce_fusion.2), kind=kLoop, calls=%fused_computation.6.clone.1 | loop fusion | flops 7861248 | bytes 6316544 | tf_op jit(solution)/shard_map/while/body/eval_jaxpr/reduce_sum | solution.py:47
  194.9 0.2 copy.77
  195.1 6.7 %fusion.37 = f32[4,3,256,128]{3,2,1,0:T(8,128)} fusion(f32[4,3,256,128]{3,2,1,0:T(8,128)} %get-tuple-element.213, bf16[512,4,128,1]{0,2,3,1:T(8,128)(2,1)S(1)} %bitcast.61, f32[4,512,256,3]{2,1,3,0:T(8,128)} %get-tuple-element.196, f32[4,3,256]{2,1,0:T(4,128)S(1)} %select_maximum_fusion.2, pred[512]{0:T(512)(128)(4,1)S(1)} %dynamic-slice_reduce_fusion.2, ...), kind=kOutput, calls=%fused_computation.11.clone.1 | convolution fusion | flops 411697152 | bytes 9986561 | tf_op jit(solution)/shard_map/while/body/eval_jaxpr/cgqk,kcd->cgqd/dot_general | solution.py:48
  201.9 1.3 constant_dynamic-slice_fusion.3
  203.4 4.2 %bitcast_reduce_fusion.2 = (f32[4,3,256]{2,1,0:T(4,128)S(1)}, f32[4,512,256,3]{2,1,3,0:T(8,128)}) fusion(pred[512]{0:T(512)(128)(4,1)S(1)} %dynamic-slice_reduce_fusion.2, bf16[512,4,128,1]{0,2,3,1:T(8,128)(2,1)S(1)} %bitcast.60, bf16[256,4,3,128]{3,0,2,1:T(8,128)(2,1)S(1)} %get-tuple-element.226), kind=kOutput, calls=%fused_computation.1.clone.1 | convolution fusion | flops 407368704 | bytes 7614976 | tf_op jit(solution)/shard_map/while/body/eval_jaxpr/qcgd,kcd->cgqk/dot_general | solution.py:40
  207.6 3.7 %fusion.35 = f32[4,3,256]{2,1,0:T(4,128)S(1)} fusion(f32[4,512,256,3]{2,1,3,0:T(8,128)} %get-tuple-element.196, f32[4,3,256]{2,1,0:T(4,128)S(1)} %select_maximum_fusion.2, pred[512]{0:T(512)(128)(4,1)S(1)} %dynamic-slice_reduce_fusion.2), kind=kLoop, calls=%fused_computation.6.clone.1 | loop fusion | flops 7861248 | bytes 6316544 | tf_op jit(solution)/shard_map/while/body/eval_jaxpr/reduce_sum | solution.py:47
  211.5 6.7 %fusion.37 = f32[4,3,256,128]{3,2,1,0:T(8,128)} fusion(f32[4,3,256,128]{3,2,1,0:T(8,128)} %get-tuple-element.213, bf16[512,4,128,1]{0,2,3,1:T(8,128)(2,1)S(1)} %bitcast.61, f32[4,512,256,3]{2,1,3,0:T(8,128)} %get-tuple-element.196, f32[4,3,256]{2,1,0:T(4,128)S(1)} %select_maximum_fusion.2, pred[512]{0:T(512)(128)(4,1)S(1)} %dynamic-slice_reduce_fusion.2, ...), kind=kOutput, calls=%fused_computation.11.clone.1 | convolution fusion | flops 411697152 | bytes 9986561 | tf_op jit(solution)/shard_map/while/body/eval_jaxpr/cgqk,kcd->cgqd/dot_general | solution.py:48
  218.3 1.3 constant_dynamic-slice_fusion.3
  219.6 0.2 copy.76
  219.8 4.2 %bitcast_reduce_fusion.2 = (f32[4,3,256]{2,1,0:T(4,128)S(1)}, f32[4,512,256,3]{2,1,3,0:T(8,128)}) fusion(pred[512]{0:T(512)(128)(4,1)S(1)} %dynamic-slice_reduce_fusion.2, bf16[512,4,128,1]{0,2,3,1:T(8,128)(2,1)S(1)} %bitcast.60, bf16[256,4,3,128]{3,0,2,1:T(8,128)(2,1)S(1)} %get-tuple-element.226), kind=kOutput, calls=%fused_computation.1.clone.1 | convolution fusion | flops 407368704 | bytes 7614976 | tf_op jit(solution)/shard_map/while/body/eval_jaxpr/qcgd,kcd->cgqk/dot_general | solution.py:40
  224.0 3.7 %fusion.35 = f32[4,3,256]{2,1,0:T(4,128)S(1)} fusion(f32[4,512,256,3]{2,1,3,0:T(8,128)} %get-tuple-element.196, f32[4,3,256]{2,1,0:T(4,128)S(1)} %select_maximum_fusion.2, pred[512]{0:T(512)(128)(4,1)S(1)} %dynamic-slice_reduce_fusion.2), kind=kLoop, calls=%fused_computation.6.clone.1 | loop fusion | flops 7861248 | bytes 6316544 | tf_op jit(solution)/shard_map/while/body/eval_jaxpr/reduce_sum | solution.py:47
  228.0 6.7 %fusion.37 = f32[4,3,256,128]{3,2,1,0:T(8,128)} fusion(f32[4,3,256,128]{3,2,1,0:T(8,128)} %get-tuple-element.213, bf16[512,4,128,1]{0,2,3,1:T(8,128)(2,1)S(1)} %bitcast.61, f32[4,512,256,3]{2,1,3,0:T(8,128)} %get-tuple-element.196, f32[4,3,256]{2,1,0:T(4,128)S(1)} %select_maximum_fusion.2, pred[512]{0:T(512)(128)(4,1)S(1)} %dynamic-slice_reduce_fusion.2, ...), kind=kOutput, calls=%fused_computation.11.clone.1 | convolution fusion | flops 411697152 | bytes 9986561 | tf_op jit(solution)/shard_map/while/body/eval_jaxpr/cgqk,kcd->cgqd/dot_general | solution.py:48
  234.7 1.3 constant_dynamic-slice_fusion.3
  236.2 4.2 %bitcast_reduce_fusion.2 = (f32[4,3,256]{2,1,0:T(4,128)S(1)}, f32[4,512,256,3]{2,1,3,0:T(8,128)}) fusion(pred[512]{0:T(512)(128)(4,1)S(1)} %dynamic-slice_reduce_fusion.2, bf16[512,4,128,1]{0,2,3,1:T(8,128)(2,1)S(1)} %bitcast.60, bf16[256,4,3,128]{3,0,2,1:T(8,128)(2,1)S(1)} %get-tuple-element.226), kind=kOutput, calls=%fused_computation.1.clone.1 | convolution fusion | flops 407368704 | bytes 7614976 | tf_op jit(solution)/shard_map/while/body/eval_jaxpr/qcgd,kcd->cgqk/dot_general | solution.py:40
  240.4 3.7 %fusion.35 = f32[4,3,256]{2,1,0:T(4,128)S(1)} fusion(f32[4,512,256,3]{2,1,3,0:T(8,128)} %get-tuple-element.196, f32[4,3,256]{2,1,0:T(4,128)S(1)} %select_maximum_fusion.2, pred[512]{0:T(512)(128)(4,1)S(1)} %dynamic-slice_reduce_fusion.2), kind=kLoop, calls=%fused_computation.6.clone.1 | loop fusion | flops 7861248 | bytes 6316544 | tf_op jit(solution)/shard_map/while/body/eval_jaxpr/reduce_sum | solution.py:47
  244.4 6.7 %fusion.37 = f32[4,3,256,128]{3,2,1,0:T(8,128)} fusion(f32[4,3,256,128]{3,2,1,0:T(8,128)} %get-tuple-element.213, bf16[512,4,128,1]{0,2,3,1:T(8,128)(2,1)S(1)} %bitcast.61, f32[4,512,256,3]{2,1,3,0:T(8,128)} %get-tuple-element.196, f32[4,3,256]{2,1,0:T(4,128)S(1)} %select_maximum_fusion.2, pred[512]{0:T(512)(128)(4,1)S(1)} %dynamic-slice_reduce_fusion.2, ...), kind=kOutput, calls=%fused_computation.11.clone.1 | convolution fusion | flops 411697152 | bytes 9986561 | tf_op jit(solution)/shard_map/while/body/eval_jaxpr/cgqk,kcd->cgqd/dot_general | solution.py:48
  251.1 1.9 copy.64
  253.2 7.6 %convolution_convert_fusion = bf16[256,3072]{1,0:T(8,128)(2,1)} fusion(bf16[256,1536]{0,1:T(8,128)(2,1)S(1)} %bitcast.62, bf16[1536,3072]{1,0:T(8,128)(2,1)} %param.15), kind=kOutput, calls=%fused_computation.22 | convolution fusion | flops 2416705536 | bytes 11796480 | tf_op jit(solution)/shard_map/dot_general | solution.py:114
  260.8 1.3 select_reduce_fusion.4
  262.1 0.6 iota_compare_fusion.3
  262.9 22.6 %reduce-scatter.2.cloned.1.call-done = bf16[128,3072]{1,0:T(8,128)(2,1)} async-done(((bf16[256,3072]{1,0:T(8,128)(2,1)}), bf16[128,3072]{1,0:T(8,128)(2,1)}) %reduce-scatter.2.cloned.1.call-update) | async-done | bytes 786448 | tf_op jit(solution)/shard_map/reduce_scatter | solution.py:113
  285.6 2.2 add_convert_fusion
  (68 shorter events, 2.9 us)
Async XLA Ops:
  6.5 20.9 %copy-start = (bf16[128,3072]{1,0:T(8,128)(2,1)S(1)}, bf16[128,3072]{1,0:T(8,128)(2,1)}, u32[]{:S(2)}) copy-start(bf16[128,3072]{1,0:T(8,128)(2,1)} %param.11) | copy-start | bytes 2359300
  6.5 25.6 %copy-start.4 = (s32[16]{0:T(128)S(1)}, s32[16]{0:T(128)}, u32[]{:S(2)}) copy-start(s32[16]{0:T(128)} %param.19) | copy-start | bytes 196
  6.5 27.0 %copy-start.3 = (s32[8,8]{1,0:T(8,128)S(1)}, s32[8,8]{1,0:T(8,128)}, u32[]{:S(2)}) copy-start(s32[8,8]{1,0:T(8,128)} %param.18) | copy-start | bytes 772
  6.5 62.4 %all-gather.3.cloned.1.call-start = ((), (), s32[]{:S(2)}) async-start(), calls=%async_computation.4 | async-start | bytes 4456448 | tf_op jit(solution)/shard_map/all_gather | solution.py:103
  17.8 102.4 %all-gather.5.cloned.1.call-start = ((), (), s32[]{:S(2)}) async-start(), calls=%async_computation.5 | async-start | bytes 4456448 | tf_op jit(solution)/shard_map/all_gather | solution.py:104
  28.6 12.0 %all-to-all-start.1 = ((bf16[128,2,1536]{0,2,1:T(8,128)(2,1)}), bf16[128,2,1536]{0,2,1:T(8,128)(2,1)S(1)}, u32[]{:S(2)}, u32[]{:S(2)}) async-start(bf16[128,2,1536]{0,2,1:T(8,128)(2,1)} %bitcast.4), calls=%async_computation.1 | async-start | bytes 1572864 | tf_op jit(solution)/shard_map/all_to_all | solution.py:90
  32.1 253.5 %reduce-scatter.2.cloned.1.call-start = ((), (), s32[]{:S(2)}) async-start(), calls=%async_computation.6 | async-start | bytes 2359296 | tf_op jit(solution)/shard_map/reduce_scatter | solution.py:113
  253.2 7.6 %copy-start.5 = (s32[8]{0:T(128)S(1)}, s32[8]{0:T(128)}, u32[]{:S(2)}) copy-start(s32[8]{0:T(128)} %param.17) | copy-start | bytes 100
  253.2 9.6 %copy-start.1 = (f32[64,3072]{1,0:T(8,128)S(1)}, f32[64,3072]{1,0:T(8,128)}, u32[]{:S(2)}) copy-start(f32[64,3072]{1,0:T(8,128)} %param.16) | copy-start | bytes 2359300
  253.2 32.3 %copy-start.2 = (bf16[128,3072]{1,0:T(8,128)(2,1)S(1)}, bf16[128,3072]{1,0:T(8,128)(2,1)}, u32[]{:S(2)}) copy-start(bf16[128,3072]{1,0:T(8,128)(2,1)} %param.14) | copy-start | bytes 2359300
Sparse Core Ops, SparseCore 0:
  17.9 50.9 all-gather.2
  71.1 49.0 all-gather.4
  260.9 24.5 reduce-scatter.1
where the time goes:
time: 295 us; the launch traced here: 294 us
  waiting for transfers between devices  102 us (35%)
  matrix products  94.4 us (32%)
  other arithmetic  36.2 us (12%)
  local copies, waits for them, and re-layouts  28.2 us (10%)
  blocking collectives  16.7 us (6%)
  between operations  13.3 us (5%)
  starting transfers between devices  3.62 us (1%)
    dot_general x8, matrix products, attend_block(): jnp.einsum('cgqk,kcd->cgqd', weights.astype(jnp.bfloat16), values_three,...  53.4 us
    all_gather x1, waiting for transfers between devices, per_device(): value_piece = lax.all_gather(local_values, 'seq', axis=0, tiled=True)  51.2 us
    dot_general x8, matrix products, attend_block(): jnp.einsum('qcgd,kcd->cgqk', grouped, keys_three, preferred_element_type=...  33.5 us
    reduce_sum x8, other arithmetic, attend_block(): weight_sum = weight_sum * factor + jnp.sum(weights, axis=-1)  29.8 us
    reduce_scatter x1, waiting for transfers between devices, per_device(): lax.psum_scatter(jnp.dot(attended, out_weight, preferred_element_type=jnp...  22.6 us
    all_gather x1, waiting for transfers between devices, per_device(): key_piece = lax.all_gather(local_keys, 'seq', axis=0, tiled=True)  21 us
    dynamic_slice x32, local copies, waits for them, and re-layouts, sweep(): return lax.scan(scan_step, state_now, stacked)[0]  13.8 us
    all_to_all x1, blocking collectives, per_device(): lax.all_to_all(key_rows, 'head', split_axis=1, concat_axis=0, tiled=True)  9.18 us
  transfers between devices with their start and end apart: 4, of which 4 were waited for; matrix products, arithmetic and copies ran while one was open for 5% of the time, Pallas kernels for 0%

commit v1 on v0

v1 whole, which is shorter than its diff:
```python
import functools
import math

import jax
import jax.numpy as jnp
from jax import lax
from jax.experimental import pallas as pl
from jax.experimental.pallas import tpu as pltpu
from jax.sharding import PartitionSpec as P

Q_HEADS = 24
KV_HEADS = 8
HEAD_DIM = 128
GROUP = Q_HEADS // KV_HEADS
CORES = 2
NEG = -1e30
SCALE = 1.4426950408889634 * HEAD_DIM ** -0.5
STAT = 8
ONES = 16
LARGE = 1e27
VMEM_LIMIT = 24 * 1024 * 1024
LITTLE = pl.CostEstimate(flops=1, bytes_accessed=1, transcendentals=0)


def grid_of(n_seq):
    chips = n_seq // CORES
    inner = 2 ** (int(math.log2(chips)) // 2)
    return chips // inner, inner


def attend_kernel(place, n_items, parts, mine, rows, tok, first, last, refs):
    own_ref, map_ref, mask_ref, qt = refs[:4]
    state_in = None if first else refs[4]
    items = refs[4 if first else 5 : -10]
    out_ref = refs[-10]
    st_s, kv_s, vt_s, list_s, land_s, full_s, count_s, top_s, sems = refs[-9:]
    st = st_s if last else out_ref
    heads = qt.shape[1]
    kv_heads = heads // GROUP
    kvw = kv_heads * HEAD_DIM
    own = own_ref[0]
    sums = slice(0, HEAD_DIM + STAT)
    weights = slice(HEAD_DIM, HEAD_DIM + STAT)
    point = slice(HEAD_DIM + STAT, HEAD_DIM + 2 * STAT)

    def copies(i, kp, ik):
        pieces = place.refs(items, i, kp)
        size = tok // len(pieces)
        return [
            pltpu.make_async_copy(piece, kv_s.at[ik, pl.ds(j * size, size)], sems.at[ik, j])
            for j, piece in enumerate(pieces)
        ]

    seg_q = [map_ref[place.query(own, j)] for j in range(parts)]
    counts = [jnp.int32(0)] * parts
    landed = jnp.int32(0)
    for i in range(n_items):
        for kp in range(parts):
            ik = i * parts + kp
            valid, src = place.source(own, i, kp)
            seg_k = map_ref[src]
            any_seen = jnp.int32(0)
            for qp in mine:
                seen = (mask_ref[seg_q[qp], seg_k] > 0).astype(jnp.int32)
                if valid is not None:
                    seen = seen * valid.astype(jnp.int32)
                list_s[qp, counts[qp]] = ik
                counts[qp] = counts[qp] + seen
                any_seen = jnp.maximum(any_seen, seen)
            land_s[landed] = ik
            landed = landed + any_seen

            @pl.when(any_seen > 0)
            def _():
                for one in copies(i, kp, ik):
                    one.start()

    ones = jnp.ones((ONES, tok), jnp.bfloat16)

    def land(t, carry):
        ik = land_s[t]
        for one in copies(0, 0, ik):
            one.wait()
        for kh in range(kv_heads):
            v = kv_s[ik, :, kvw + kh * HEAD_DIM : kvw + (kh + 1) * HEAD_DIM]
            vt_s[ik, kh, :HEAD_DIM] = v.astype(jnp.float32).T.astype(jnp.bfloat16)
            vt_s[ik, kh, HEAD_DIM:] = ones
        return carry

    lax.fori_loop(0, landed, land, 0)

    def blocks(qp, t):
        single = 2 * t + 1 >= full_s[qp]
        i0 = list_s[qp, 2 * t]
        i1 = list_s[qp, jnp.where(single, 2 * t, 2 * t + 1)]
        return i0, i1, jnp.where(single, jnp.float32(NEG), jnp.float32(0.0))

    def scores(qp, h, i0, i1):
        lanes = slice((h // GROUP) * HEAD_DIM, (h // GROUP + 1) * HEAD_DIM)
        k = jnp.concatenate([kv_s[i0, :, lanes], kv_s[i1, :, lanes]], axis=0)
        s = jnp.dot(k, qt[qp, h], preferred_element_type=jnp.float32)
        return s.reshape(2, tok // STAT, STAT, rows) * SCALE

    def product(h, i0, i1, s, ref0, ref1):
        p0 = jnp.exp2(s[0] - ref0[None]).reshape(tok, rows).astype(jnp.bfloat16)
        p1 = jnp.exp2(s[1] - ref1[None]).reshape(tok, rows).astype(jnp.bfloat16)
        vt = jnp.concatenate([vt_s[i0, h // GROUP], vt_s[i1, h // GROUP]], axis=1)
        pv = jnp.dot(vt, jnp.concatenate([p0, p1], axis=0), preferred_element_type=jnp.float32)
        return pv[sums]

    def slow(qp, t):
        i0, i1, bias = blocks(qp, t)
        for h in range(heads):
            s = scores(qp, h, i0, i1)
            before = st[qp, h, point]
            top = jnp.maximum(jnp.max(s[0], axis=0), jnp.max(s[1], axis=0) + bias)
            now = jnp.maximum(before, jnp.max(top, axis=0, keepdims=True))
            pv = product(h, i0, i1, s, now, now - bias)
            kept = st[qp, h, sums].reshape(-1, STAT, rows) * jnp.exp2(before - now)[None]
            st[qp, h, sums] = kept.reshape(-1, rows) + pv
            st[qp, h, point] = now

    def fast(qp, t):
        i0, i1, bias = blocks(qp, t)
        old = [st[qp, h] for h in range(heads)]
        new = []
        for h in range(heads):
            ref = old[h][point]
            new.append(old[h][sums] + product(h, i0, i1, scores(qp, h, i0, i1), ref, ref - bias))
        for h in range(heads):
            st[qp, h, sums] = new[h]

    for qp in mine:
        full_s[qp] = counts[qp]
        count_s[qp] = (counts[qp] + 1) // 2

    def attempt(again, carry):
        @pl.when(jnp.logical_or(again == 0, top_s[0] > 0))
        def _():
            for qp in mine:
                for h in range(heads):
                    if first:
                        st[qp, h, sums] = jnp.zeros((HEAD_DIM + STAT, rows), jnp.float32)
                        st[qp, h, point] = jnp.full((STAT, rows), NEG, jnp.float32)
                    else:
                        st[qp, h] = state_in[qp, h]

            def one_part(qp, carry):
                pairs = count_s[qp]
                switch = jnp.where(again > 0, pairs, 1 if first else 0)

                def one_slow(t, carry):
                    slow(qp, t)
                    return carry

                def one_fast(t, carry):
                    fast(qp, t)
                    return carry

                lax.fori_loop(0, switch, one_slow, 0)
                lax.fori_loop(switch, pairs, one_fast, 0)
                return carry

            lax.fori_loop(mine[0], mine[-1] + 1, one_part, 0)
            top = jnp.zeros((STAT, rows), jnp.float32)
            for qp in mine:
                for h in range(heads):
                    top = jnp.maximum(top, jnp.where(st[qp, h, weights] < LARGE, 0.0, 1.0))
            top_s[0] = (jnp.max(top) > 0.0).astype(jnp.int32)

        return carry

    top_s[0] = 0
    lax.fori_loop(0, 2, attempt, 0)
    if last:
        for j, qp in enumerate(mine):
            for h in range(heads):
                inv = 1.0 / st[qp, h, weights]
                att = st[qp, h, :HEAD_DIM].reshape(-1, STAT, rows) * inv[None]
                out_ref[j * rows : (j + 1) * rows, h * HEAD_DIM : (h + 1) * HEAD_DIM] = (
                    att.reshape(HEAD_DIM, rows).T.astype(jnp.bfloat16)
                )


class GridPlace:
    def __init__(self, metas, n_a, n_b):
        self.metas, self.n_a, self.n_b = metas, n_a, n_b

    def query(self, own, part):
        return (own // CORES) * CORES + (own % CORES + part) % CORES

    def source(self, own, i, part):
        flip, db, only, _ = self.metas[i]
        a, b, c = own // (CORES * self.n_b), (own // CORES) % self.n_b, own % CORES
        valid = None
        if len(only) < self.n_a:
            valid = functools.reduce(jnp.logical_or, [a == one for one in only])
        return valid, ((a ^ flip) * self.n_b + (b + db) % self.n_b) * CORES + (c + part) % CORES

    def refs(self, items, i, part):
        first = sum(len(meta[3]) for meta in self.metas[:i])
        out = []
        for ref, halves in zip(items[first:], self.metas[i][3]):
            rows = ref.shape[0] // (CORES * halves)
            out += [ref.at[pl.ds((half * CORES + part) * rows, rows)] for half in range(halves)]
        return out


class FlatPlace:
    def __init__(self, tok):
        self.tok = tok

    def query(self, own, part):
        return own

    def source(self, own, i, part):
        return None, i

    def refs(self, items, i, part):
        return [items[0].at[pl.ds(i * self.tok, self.tok)]]


def other_columns(own, pieces):
    rows, width = pieces[0].shape
    half = width // CORES
    vmem = pl.BlockSpec(memory_space=pltpu.VMEM)

    def kernel(own_ref, *refs):
        lanes = pl.ds(pl.multiple_of((own_ref[0] + 1) % CORES * half, half), half)
        for i, ref in enumerate(refs[:-1]):
            refs[-1][i * rows : (i + 1) * rows] = ref[:, lanes]

    return pl.pallas_call(
        kernel,
        out_shape=jax.ShapeDtypeStruct((len(pieces) * rows, half), pieces[0].dtype),
        in_specs=[pl.BlockSpec(memory_space=pltpu.SMEM)] + [vmem] * len(pieces),
        out_specs=vmem,
        compiler_params=pltpu.CompilerParams(vmem_limit_bytes=VMEM_LIMIT),
        cost_estimate=LITTLE,
        name="other_columns",
    )(own, *pieces)


def turn(own, parts):
    pieces = [x for part in parts for x in part]
    heads = min(x.shape[1] for x in pieces) // HEAD_DIM
    rows = sum(x.shape[0] for x in parts[0])
    vmem = pl.BlockSpec(memory_space=pltpu.VMEM)

    def kernel(own_ref, *refs):
        begin = own_ref[0] % CORES * heads * HEAD_DIM
        at = 0
        for qp, part in enumerate(parts):
            some = refs[at : at + len(part)]
            at += len(part)
            for h in range(heads):
                turned = []
                for ref in some:
                    first = h * HEAD_DIM
                    if ref.shape[1] > heads * HEAD_DIM:
                        first = pl.multiple_of(begin + first, HEAD_DIM)
                    turned.append(ref[:, pl.ds(first, HEAD_DIM)].astype(jnp.float32).T)
                refs[-1][qp, h] = jnp.concatenate(turned, axis=1).astype(jnp.bfloat16)

    return pl.pallas_call(
        kernel,
        out_shape=pltpu.VMEM((len(parts), heads, HEAD_DIM, rows), jnp.bfloat16),
        in_specs=[pl.BlockSpec(memory_space=pltpu.SMEM)] + [vmem] * len(pieces),
        out_specs=vmem,
        compiler_params=pltpu.CompilerParams(vmem_limit_bytes=VMEM_LIMIT),
        cost_estimate=LITTLE,
        name="turn",
    )(own, *pieces)


def attend(scalars, q, state, arrays, place, n_items, parts, tok, last, mine=None):
    mine = tuple(range(parts)) if mine is None else mine
    first = state is None
    heads, rows = q.shape[1], q.shape[3]
    width = arrays[0].shape[1]
    smem = pl.BlockSpec(memory_space=pltpu.SMEM)
    vmem = pl.BlockSpec(memory_space=pltpu.VMEM)
    args = list(scalars) + [pinned(q)] + ([] if first else [pinned(state)]) + list(arrays)
    specs = [smem] * 3 + [vmem] + ([] if first else [vmem])
    specs += [pl.BlockSpec(memory_space=pl.ANY)] * len(arrays)
    shape = (parts, heads, HEAD_DIM + 2 * STAT, rows)
    blocks = n_items * parts
    scratch = [
        pltpu.VMEM(shape if last else (STAT, HEAD_DIM), jnp.float32),
        pltpu.VMEM((blocks, tok, width), jnp.bfloat16),
        pltpu.VMEM((blocks, heads // GROUP, HEAD_DIM + ONES, tok), jnp.bfloat16),
        pltpu.SMEM((parts, blocks + 1), jnp.int32),
        pltpu.SMEM((blocks + 1,), jnp.int32),
        pltpu.SMEM((parts,), jnp.int32),
        pltpu.SMEM((parts,), jnp.int32),
        pltpu.SMEM((1,), jnp.int32),
        pltpu.SemaphoreType.DMA((blocks, 2)),
    ]
    if last:
        out_shape = [jax.ShapeDtypeStruct((len(mine) * rows, heads * HEAD_DIM), jnp.bfloat16)]
    else:
        out_shape = [pltpu.VMEM(shape, jnp.float32)]

    def kernel(*refs):
        attend_kernel(place, n_items, parts, mine, rows, tok, first, last, refs)

    return pl.pallas_call(
        kernel,
        out_shape=out_shape,
        in_specs=specs,
        out_specs=[vmem] * len(out_shape),
        scratch_shapes=scratch,
        compiler_params=pltpu.CompilerParams(vmem_limit_bytes=VMEM_LIMIT),
        cost_estimate=LITTLE,
        name="attend",
    )(*args)


def pinned(x):
    return pltpu.with_memory_space_constraint(x, pltpu.VMEM)


def fetch(weight):
    chunks = 12
    rows = weight.shape[0] // chunks

    def kernel(weight_ref, out_ref, sems):
        copies = [
            pltpu.make_async_copy(
                weight_ref.at[pl.ds(i * rows, rows)], out_ref.at[pl.ds(i * rows, rows)], sems.at[i]
            )
            for i in range(chunks)
        ]
        for one in copies:
            one.start()
        for one in copies:
            one.wait()

    return pl.pallas_call(
        kernel,
        out_shape=pltpu.VMEM(weight.shape, weight.dtype),
        in_specs=[pl.BlockSpec(memory_space=pltpu.HBM)],
        out_specs=pl.BlockSpec(memory_space=pltpu.VMEM),
        scratch_shapes=[pltpu.SemaphoreType.DMA((chunks,))],
        compiler_params=pltpu.CompilerParams(vmem_limit_bytes=VMEM_LIMIT),
        cost_estimate=LITTLE,
        name="fetch",
    )(pltpu.with_memory_space_constraint(weight, pltpu.HBM))


def project(own, parts, weight, rows, partial=None, ending=None):
    width = weight.shape[1]
    depth = parts[0][0].shape[1]
    tile = math.gcd(width, 512)
    smem = pl.BlockSpec(memory_space=pltpu.SMEM)
    vmem = pl.BlockSpec(memory_space=pltpu.VMEM)
    n = len(parts)
    args = [own] + [x for x, _, _ in parts] + [pinned(weight)]
    specs = [smem] + [vmem] * (n + 1)
    scratch = []
    out_shape = [jax.ShapeDtypeStruct((rows, width), jnp.bfloat16)]
    if partial is not None:
        args.append(pinned(partial))
        specs.append(vmem)
    elif ending is not None:
        args += list(ending)
        args[-2] = pltpu.with_memory_space_constraint(args[-2], pltpu.HBM)
        specs += [smem] * 2 + [pl.BlockSpec(memory_space=pltpu.HBM), vmem]
        out_shape = [pltpu.VMEM((rows, width), jnp.float32), pltpu.VMEM((STAT, width), jnp.float32)]
        scratch = [pltpu.VMEM((STAT, width), jnp.float32), pltpu.SemaphoreType.DMA]
    else:
        out_shape = [pltpu.VMEM((rows, width), jnp.float32)]

    def kernel(*refs):
        own_ref, part_refs, weight_ref, refs = refs[0], refs[1 : n + 1], refs[n + 1], refs[n + 2 :]
        if ending is not None:
            steps_ref, map_ref, gate_ref, residual_ref, out_ref, row_ref, near, sem = refs
            step = steps_ref[map_ref[own_ref[0]]]
            copy = pltpu.make_async_copy(
                gate_ref.at[pl.ds(pl.multiple_of((step // STAT) * STAT, STAT), STAT)], near, sem
            )
            copy.start()
            copy.wait()
            chosen = lax.broadcasted_iota(jnp.int32, (STAT, width), 0) == step % STAT
            row = jnp.sum(jnp.where(chosen, near[...], 0.0), axis=0, keepdims=True)
            row_ref[...] = jnp.broadcast_to(row, (STAT, width))
        else:
            out_ref = refs[-1]

        def one(t, carry):
            lanes = pl.ds(pl.multiple_of(t * tile, tile), tile)
            total = None
            for j in range(n):
                first_row = parts[j][2]
                group = (own_ref[0] + parts[j][1]) % CORES
                weight_rows = pl.ds(pl.multiple_of(group * depth, depth), depth)
                term = jnp.dot(
                    part_refs[j][first_row : first_row + rows],
                    weight_ref[weight_rows, lanes],
                    preferred_element_type=jnp.float32,
                )
                total = term if total is None else total + term
            if partial is not None:
                total = total + refs[0][:, lanes]
            if ending is not None:
                gate = jnp.concatenate([row_ref[:, lanes]] * (rows // STAT), axis=0)
                total = residual_ref[:, lanes].astype(jnp.float32) + gate * total
            out_ref[:, lanes] = total.astype(out_ref.dtype)
            return carry

        lax.fori_loop(0, width // tile, one, 0)

    return pl.pallas_call(
        kernel,
        out_shape=out_shape,
        in_specs=specs,
        out_specs=[vmem] * len(out_shape),
        scratch_shapes=scratch,
        compiler_params=pltpu.CompilerParams(vmem_limit_bytes=VMEM_LIMIT),
        cost_estimate=pl.CostEstimate(
            flops=2 * rows * depth * n * width, bytes_accessed=2 * depth * n * width, transcendentals=0
        ),
        name="project",
    )(*args)


def columns(x, part, width):
    return lax.dynamic_slice_in_dim(x, part * width, width, 1)


def paired(query_rows, key_rows, value_rows, out_weight, scalars, ending, n_a, n_b):
    n_seq = n_a * n_b * CORES
    groups = 2 * CORES
    own = scalars[0]
    kvw = key_rows.shape[1] // groups
    rows = query_rows.shape[0]
    tok = 2 * rows
    x = lax.axis_index("head")
    c = lax.axis_index("seq") % CORES

    def index(a, b, k):
        return (a * n_b + b) * CORES + k

    def swapped(piece, dx, dc):
        pairs = [
            ((s ^ dc) * 2 + (h ^ dx), s * 2 + h) for s in range(n_seq) for h in range(2)
        ]
        return lax.ppermute(piece, ("seq", "head"), pairs)

    def along_a(piece, moves):
        pairs = [
            (index(a, b, k), index(to, b, k)) for a, to in moves for b in range(n_b) for k in range(CORES)
        ]
        return lax.ppermute(piece, "seq", pairs)

    def beside_of(piece, only):
        pairs = [
            (index(a, 1 - b, k), index(a, b, k)) for a in only for b in range(n_b) for k in range(CORES)
        ]
        return lax.ppermute(piece, "seq", pairs)

    def stage(state, q, waiting, last=False, mine=None):
        return attend(
            scalars, q, state, [x for w, _ in waiting for x in w], GridPlace([m for _, m in waiting], n_a, n_b),
            len(waiting), CORES, tok, last, mine,
        )

    def kv_for(dx, dc):
        j = (x ^ dx) * CORES + (c ^ dc)
        return jnp.concatenate([columns(key_rows, j, kvw), columns(value_rows, j, kvw)], axis=1)

    ends, middle, chips = [0, 3], [1, 2], list(range(n_a))
    order = [(0, 0), (1, 0), (0, 1), (1, 1)]
    pieces = {d: kv_for(*d) if sum(d) == 0 else swapped(kv_for(*d), *d) for d in order}
    early = jnp.concatenate([pieces[0, 0], pieces[0, 1]], axis=0)
    later = jnp.concatenate([pieces[1, 0], pieces[1, 1]], axis=0)
    next_early = along_a(early, [(a, a ^ 1) for a in chips])
    block = jnp.concatenate([early, later], axis=0)
    qw = query_rows.shape[1] // 2
    q_own, q_other = columns(query_rows, x, qw), columns(query_rows, 1 - x, qw)
    block, later, out_weight, q_own, q_other = lax.optimization_barrier(
        (block, later, out_weight, q_own, q_other)
    )
    beside = beside_of(block, chips)
    far = along_a(block, [(a, a ^ 2) for a in chips])
    next_later = along_a(later, [(a, a ^ 1) for a in chips])
    q_came = swapped(q_other, 1, 0)
    weight = fetch(out_weight)
    q_came, weight = lax.optimization_barrier((q_came, weight))
    q_core = swapped(other_columns(own, [q_own, q_came]), 0, 1)
    q = turn(own, [[q_own, q_came], [q_core]])
    beside_early = beside_of(next_early, chips)
    (state,) = stage(None, q, [([block], (0, 0, chips, [2])), ([beside], (0, 1, chips, [2]))])
    next_later, beside_early, state = lax.optimization_barrier((next_later, beside_early, state))
    beside_later = beside_of(next_later, chips)
    far, again, state = lax.optimization_barrier((far, block, state))
    to_ends = along_a(far, [(1, 0), (2, 3)])
    beside_far = beside_of(far, chips)
    to_middle = along_a(again, [(1, 2), (2, 1)])
    (state,) = stage(state, q, [([next_early, next_later], (1, 0, chips, [1, 1])), ([far], (2, 0, chips, [2]))])
    (state,) = stage(state, q, [([beside_early, beside_later], (1, 1, chips, [1, 1]))])
    to_ends, to_middle, state = lax.optimization_barrier((to_ends, to_middle, state))
    beside_last = [
        ([beside_of(to_ends, ends)], (3, 1, ends, [2])),
        ([beside_of(to_middle, middle)], (3, 1, middle, [2])),
    ]
    last = [([to_ends], (3, 0, ends, [2])), ([to_middle], (3, 0, middle, [2]))]
    (state,) = stage(state, q, [([beside_far], (2, 1, chips, [2]))] + last)
    (sent,) = stage(state, q, beside_last, True, (1,))
    came = swapped(sent, 0, 1)
    state, sent = lax.optimization_barrier((state, sent))
    (kept,) = stage(state, q, beside_last, True, (0,))
    (begun,) = project(own, [(kept, 0, rows)], weight, rows)
    (theirs,) = project(own, [(came, 1, rows)], weight, rows, partial=begun)
    came_back = lax.ppermute(theirs, "head", [(0, 1), (1, 0)])
    base, gate = project(own, [(kept, 0, 0), (came, 1, 0)], weight, rows, ending=ending)
    return (base + gate[:1] * came_back.astype(jnp.float32)).astype(jnp.bfloat16)


def gathered_attention(query_rows, key_rows, value_rows, scalars):
    spread = functools.partial(lax.all_to_all, axis_name="head", split_axis=1, concat_axis=0, tiled=True)
    local = jnp.concatenate([spread(key_rows), spread(value_rows)], axis=1)
    every = lax.all_gather(local, "seq", axis=0, tiled=True)
    tok = local.shape[0]
    return attend(
        scalars, turn(scalars[0], [[spread(query_rows)]]), None, [every], FlatPlace(tok), every.shape[0] // tok, 1, tok, True
    )[0]


def per_device(
    query_rows,
    key_rows,
    value_rows,
    residual,
    out_weight,
    gate_table,
    noise_steps,
    segment_mask,
    segment_map,
):
    n_seq = lax.axis_size("seq")
    n_head = lax.axis_size("head")
    own_seq = lax.axis_index("seq").astype(jnp.int32)
    own = own_seq.reshape(1)
    scalars = (own, segment_map, segment_mask)
    n_a, n_b = grid_of(n_seq)
    if n_head == 2 and n_a == 4 and n_b == 2:
        ending = (noise_steps, segment_map, gate_table, residual)
        return paired(query_rows, key_rows, value_rows, out_weight, scalars, ending, n_a, n_b)
    attended = gathered_attention(query_rows, key_rows, value_rows, scalars)
    projected = lax.psum_scatter(
        jnp.dot(attended, out_weight, preferred_element_type=jnp.float32).astype(jnp.bfloat16),
        "head",
        scatter_dimension=0,
        tiled=True,
    ).astype(jnp.float32)
    gate_row = lax.dynamic_slice_in_dim(gate_table, noise_steps[segment_map[own_seq]], 1, 0)
    return (residual.astype(jnp.float32) + gate_row * projected).astype(jnp.bfloat16)


def solution(mesh):
    placed = (
        P(("seq", "head"), None),
        P(("seq", "head"), None),
        P(("seq", "head"), None),
        P(("seq", "head"), None),
        P("head", None),
        P(),
        P(),
        P(),
        P(),
    )
    return jax.shard_map(
        per_device, mesh=mesh, in_specs=placed, out_specs=P(("seq", "head"), None), check_vma=False
    )
```

time: 295 us -> 106 us (0.36)
  the two profiles are of different devices: /device:TPU:0 before, /device:TPU:12 now
where the time goes in v1:
time: 106 us; the launch traced here: 105 us
  waiting for transfers between devices  46 us (43%)
  Pallas kernels  33.5 us (32%)
  starting transfers between devices  23.3 us (22%)
  local copies, waits for them, and re-layouts  1.26 us (1%)
  other arithmetic  1.2 us (1%)
    pallas_call x6, Pallas kernels, attend(): pl.pallas_call(kernel, out_shape=out_shape, in_specs=specs, out_specs=[vm...  22 us
    ppermute x1, waiting for transfers between devices, paired(): came_back = lax.ppermute(theirs, 'head', [(0, 1), (1, 0)])  15.9 us
    ppermute x6, waiting for transfers between devices, beside_of(): return lax.ppermute(piece, 'seq', pairs)  14.7 us
    ppermute x5, starting transfers between devices, along_a(): return lax.ppermute(piece, 'seq', pairs)  11.4 us
    ppermute x6, starting transfers between devices, beside_of(): return lax.ppermute(piece, 'seq', pairs)  8.23 us
    ppermute x6, waiting for transfers between devices, swapped(): return lax.ppermute(piece, ('seq', 'head'), pairs)  8.08 us
    pallas_call x3, Pallas kernels, project(): pl.pallas_call(kernel, out_shape=out_shape, in_specs=specs, out_specs=[vm...  7.37 us
    ppermute x5, waiting for transfers between devices, along_a(): return lax.ppermute(piece, 'seq', pairs)  7.24 us
  transfers between devices with their start and end apart: 18, of which 11 were waited for; matrix products, arithmetic and copies ran while one was open for 0% of the time, Pallas kernels for 27%

profile of v1, /device:TPU:12, one launch (start us, length us, event | category | flops | bytes accessed | tf_op | source)
XLA Modules:
  0.0 105.4 jit_solution(5621319410877023092)
XLA Ops:
  0.0 0.0 copy-start.4
  0.0 1.2 %constant_dynamic-slice_fusion.8 = (bf16[128,256]{1,0:T(8,128)(2,1)S(1)}, bf16[128,256]{1,0:T(8,128)(2,1)S(1)}, bf16[128,256]{1,0:T(8,128)(2,1)S(1)}, bf16[128,2...) fusion(bf16[128,1024]{1,0:T(8,128)(2,1)} %param.11, ...), kind=kLoop, calls=%fused_computation.15 | loop fusion | bytes 1048592 | tf_op jit(solution)/shard_map/dynamic_slice | solution.py:428
  1.2 1.6 %collective-permute-start.1 = (bf16[128,512]{1,0:T(8,128)(2,1)S(1)}, bf16[128,512]{1,0:T(8,128)(2,1)S(1)}, u32[]{:S(2)}, u32[]{:S(2)}) collective-permute-start(bf16[128,512]{1,0:T(8,128)(2,1)S(1)} %pad_maximum_fusion.4), channel_id=1, source_target_pairs={{1,0},{0,1},{3,2},{2,3},{5,4},{4,5},{7,6},{6,7},{9,8},{8,9},{11,10... | collective-permute-start | bytes 393224 | tf_op jit(solution)/shard_map/ppermute | solution.py:448
  2.8 0.1 collective-permute-start.2
  2.9 0.7 collective-permute-start
  3.6 0.0 copy-done.4
  3.6 0.1 constant_dynamic-slice_fusion
  3.6 3.6 %collective-permute-done.1 = bf16[128,512]{1,0:T(8,128)(2,1)S(1)} collective-permute-done((bf16[128,512]{1,0:T(8,128)(2,1)S(1)}, bf16[128,512]{1,0:T(8,128)(2,1)S(1)}, u32[]{:S(2)}, u32[]{:S(2)}) %collective-permute-start.1) | collective-permute-done | bytes 131104 | tf_op jit(solution)/shard_map/ppermute | solution.py:448
  7.2 1.4 %collective-permute-done.2 = bf16[128,512]{1,0:T(8,128)(2,1)S(1)} collective-permute-done((bf16[128,512]{1,0:T(8,128)(2,1)S(1)}, bf16[128,512]{1,0:T(8,128)(2,1)S(1)}, u32[]{:S(2)}, u32[]{:S(2)}) %collective-permute-start.2) | collective-permute-done | bytes 131104 | tf_op jit(solution)/shard_map/ppermute | solution.py:448
  8.6 0.0 collective-permute-done
  8.7 1.1 %collective-permute-start.3 = (bf16[128,1536]{1,0:T(8,128)(2,1)S(1)}, bf16[128,1536]{1,0:T(8,128)(2,1)S(1)}, u32[]{:S(2)}, u32[]{:S(2)}) collective-permute-start(bf16[128,1536]{1,0:T(8,128)(2,1)S(1)} %get-tuple-element.25), channel_id=1, source_target_pairs={{1,0},{0,1},{3,2},{2,3},{5,4},{4,5},{7,6},{6,7},{9,8},{8,9},{11,10... | collective-permute-start | bytes 1179656 | tf_op jit(solution)/shard_map/ppermute | solution.py:448
  9.8 0.5 collective-permute-start.9
  10.3 0.5 collective-permute-start.7
  10.8 2.6 %collective-permute-start.5 = (bf16[512,512]{1,0:T(8,128)(2,1)S(1)}, bf16[512,512]{1,0:T(8,128)(2,1)S(1)}, u32[]{:S(2)}, u32[]{:S(2)}) collective-permute-start(bf16[512,512]{1,0:T(8,128)(2,1)S(1)} %pad_maximum_fusion.refs_4_), channel_id=1, source_target_pairs={{0,16},{2,18},{4,20},{6,22},{8,24},{10,26},{12,28},{14,30},{16,0},... | collective-permute-start | bytes 1572872 | tf_op jit(solution)/shard_map/ppermute | solution.py:454
  13.4 3.8 %fetch.1.refs_3_.refs_2_ = bf16[1536,3072]{1,0:T(8,128)(2,1)S(1)} custom-call(bf16[1536,3072]{1,0:T(8,128)(2,1)} %weight_ref), custom_call_target="tpu_custom_call" | custom-call | flops 1 | bytes 1 | tf_op jit(solution)/shard_map/fetch/pallas_call | solution.py:339
  17.2 3.1 %collective-permute-done.3.refs_1_ = bf16[128,1536]{1,0:T(8,128)(2,1)S(1)} collective-permute-done((bf16[128,1536]{1,0:T(8,128)(2,1)S(1)}, bf16[128,1536]{1,0:T(8,128)(2,1)S(1)}, u32[]{:S(2)}, u32[]{:S(2)}) %collective-permute-start.3) | collective-permute-done | bytes 393248 | tf_op jit(solution)/shard_map/ppermute | solution.py:448
  20.3 0.0 copy-start.1
  20.3 0.0 copy-start.2
  20.3 0.1 collective-permute-start.4
  20.4 0.5 collective-permute-start.6
  20.9 2.0 %collective-permute-done.7.refs_5_ = bf16[256,512]{1,0:T(8,128)(2,1)S(1)} collective-permute-done((bf16[256,512]{1,0:T(8,128)(2,1)S(1)}, bf16[256,512]{1,0:T(8,128)(2,1)S(1)}, u32[]{:S(2)}, u32[]{:S(2)}) %collective-permute-start.7) | collective-permute-done | bytes 262176 | tf_op jit(solution)/shard_map/ppermute | solution.py:454
  23.0 1.5 %collective-permute-start.8 = (bf16[256,512]{1,0:T(8,128)(2,1)S(1)}, bf16[256,512]{1,0:T(8,128)(2,1)S(1)}, u32[]{:S(2)}, u32[]{:S(2)}) collective-permute-start(bf16[256,512]{1,0:T(8,128)(2,1)S(1)} %collective-permute-done.7.refs_5_), channel_id=1, source_target_pairs={{4,0},{6,2},{0,4},{2,6},{12,8},{14,10},{8,12},{10,14},{20,16},{22,... | collective-permute-start | bytes 786440 | tf_op jit(solution)/shard_map/ppermute | solution.py:460
  24.5 0.0 collective-permute-done.4.refs_2_
  24.5 0.3 turn.1.refs_3_
  24.8 0.0 collective-permute-done.9.refs_5_
  24.8 0.0 copy-done.1
  24.8 0.0 copy-done.2
  24.8 7.0 %attend.6.refs_4_ = f32[2,6,144,256]{3,2,1,0:T(8,128)S(1)} custom-call(s32[1]{0:T(128)} %bitcast.own_ref.refs_0_, s32[16]{0:T(128)S(1)} %copy-done.2, s32[8,8]{1,0:T(8,128)S(1)} %copy-done.1, bf16[2,6,128,256]{3,2,1,0:T(8,128)(2,1)S(1)} %turn.1.refs_3_, bf16[512,512]{1,0:T(8,128)(2,1)S(1)} %pad_maximum_fusion.refs_4_, ...), custom_call_target="tpu_custom_call" | custom-call | flops 1 | bytes 1 | tf_op jit(solution)/shard_map/attend/pallas_call | solution.py:307
  31.8 4.2 %collective-permute-done.6.refs_6_ = bf16[256,512]{1,0:T(8,128)(2,1)S(1)} collective-permute-done((bf16[256,512]{1,0:T(8,128)(2,1)S(1)}, bf16[256,512]{1,0:T(8,128)(2,1)S(1)}, u32[]{:S(2)}, u32[]{:S(2)}) %collective-permute-start.6) | collective-permute-done | bytes 262176 | tf_op jit(solution)/shard_map/ppermute | solution.py:454
  35.9 0.0 collective-permute-done.8.refs_5_
  35.9 0.3 collective-permute-done.5.refs_7_
  36.2 4.3 %collective-permute-start.10 = (bf16[512,512]{1,0:T(8,128)(2,1)S(1)}, bf16[512,512]{1,0:T(8,128)(2,1)S(1)}, u32[]{:S(2)}, u32[]{:S(2)}) collective-permute-start(bf16[512,512]{1,0:T(8,128)(2,1)S(1)} %collective-permute-done.5.refs_7_), channel_id=1, source_target_pairs={{8,0},{10,2},{12,4},{14,6},{16,24},{18,26},{20,28},{22,30},{9,1},{... | collective-permute-start | bytes 1572872 | tf_op jit(solution)/shard_map/ppermute | solution.py:454
  40.5 3.5 %collective-permute-start.11 = (bf16[512,512]{1,0:T(8,128)(2,1)S(1)}, bf16[512,512]{1,0:T(8,128)(2,1)S(1)}, u32[]{:S(2)}, u32[]{:S(2)}) collective-permute-start(bf16[512,512]{1,0:T(8,128)(2,1)S(1)} %pad_maximum_fusion.refs_4_), channel_id=1, source_target_pairs={{8,16},{10,18},{12,20},{14,22},{16,8},{18,10},{20,12},{22,14},{9,1... | collective-permute-start | bytes 1572872 | tf_op jit(solution)/shard_map/ppermute | solution.py:454
  44.0 1.6 %collective-permute-start.12 = (bf16[256,512]{1,0:T(8,128)(2,1)S(1)}, bf16[256,512]{1,0:T(8,128)(2,1)S(1)}, u32[]{:S(2)}, u32[]{:S(2)}) collective-permute-start(bf16[256,512]{1,0:T(8,128)(2,1)S(1)} %collective-permute-done.6.refs_6_), channel_id=1, source_target_pairs={{4,0},{6,2},{0,4},{2,6},{12,8},{14,10},{8,12},{10,14},{20,16},{22,... | collective-permute-start | bytes 786440 | tf_op jit(solution)/shard_map/ppermute | solution.py:460
  45.6 0.5 collective-permute-start.13
  46.1 5.4 %attend.7.refs_4_ = f32[2,6,144,256]{3,2,1,0:T(8,128)S(1)} custom-call(s32[1]{0:T(128)} %bitcast.own_ref.refs_0_, s32[16]{0:T(128)S(1)} %copy-done.2, s32[8,8]{1,0:T(8,128)S(1)} %copy-done.1, bf16[2,6,128,256]{3,2,1,0:T(8,128)(2,1)S(1)} %turn.1.refs_3_, f32[2,6,144,256]{3,2,1,0:T(8,128)S(1)} %attend.6.refs_4_, ...), custom_call_target="tpu_custom_call" | custom-call | flops 1 | bytes 1 | tf_op jit(solution)/shard_map/attend/pallas_call | solution.py:307
  51.5 1.8 %collective-permute-done.12.refs_6_ = bf16[256,512]{1,0:T(8,128)(2,1)S(1)} collective-permute-done((bf16[256,512]{1,0:T(8,128)(2,1)S(1)}, bf16[256,512]{1,0:T(8,128)(2,1)S(1)}, u32[]{:S(2)}, u32[]{:S(2)}) %collective-permute-start.12) | collective-permute-done | bytes 262176 | tf_op jit(solution)/shard_map/ppermute | solution.py:460
  53.3 1.2 %attend.8.refs_4_ = f32[2,6,144,256]{3,2,1,0:T(8,128)S(1)} custom-call(s32[1]{0:T(128)} %bitcast.own_ref.refs_0_, s32[16]{0:T(128)S(1)} %copy-done.2, s32[8,8]{1,0:T(8,128)S(1)} %copy-done.1, bf16[2,6,128,256]{3,2,1,0:T(8,128)(2,1)S(1)} %turn.1.refs_3_, f32[2,6,144,256]{3,2,1,0:T(8,128)S(1)} %attend.7.refs_4_, ...), custom_call_target="tpu_custom_call" | custom-call | flops 1 | bytes 1 | tf_op jit(solution)/shard_map/attend/pallas_call | solution.py:307
  54.5 0.0 collective-permute-done.10.refs_6_
  54.5 0.8 collective-permute-done.11.refs_7_
  55.3 0.7 collective-permute-start.14
  56.0 3.4 %collective-permute-start.15 = (bf16[512,512]{1,0:T(8,128)(2,1)S(1)}, bf16[512,512]{1,0:T(8,128)(2,1)S(1)}, u32[]{:S(2)}, u32[]{:S(2)}) collective-permute-start(bf16[512,512]{1,0:T(8,128)(2,1)S(1)} %collective-permute-done.11.refs_7_), channel_id=1, source_target_pairs={{12,8},{14,10},{8,12},{10,14},{20,16},{22,18},{16,20},{18,22},{13,... | collective-permute-start | bytes 1572872 | tf_op jit(solution)/shard_map/ppermute | solution.py:460
  59.4 5.1 %collective-permute-done.13.refs_5_ = bf16[512,512]{1,0:T(8,128)(2,1)S(1)} collective-permute-done((bf16[512,512]{1,0:T(8,128)(2,1)S(1)}, bf16[512,512]{1,0:T(8,128)(2,1)S(1)}, u32[]{:S(2)}, u32[]{:S(2)}) %collective-permute-start.13) | collective-permute-done | bytes 524320 | tf_op jit(solution)/shard_map/ppermute | solution.py:460
  64.5 1.2 %attend.9.refs_4_ = f32[2,6,144,256]{3,2,1,0:T(8,128)S(1)} custom-call(s32[1]{0:T(128)} %bitcast.own_ref.refs_0_, s32[16]{0:T(128)S(1)} %copy-done.2, s32[8,8]{1,0:T(8,128)S(1)} %copy-done.1, bf16[2,6,128,256]{3,2,1,0:T(8,128)(2,1)S(1)} %turn.1.refs_3_, f32[2,6,144,256]{3,2,1,0:T(8,128)S(1)} %attend.8.refs_4_, ...), custom_call_target="tpu_custom_call" | custom-call | flops 1 | bytes 1 | tf_op jit(solution)/shard_map/attend/pallas_call | solution.py:307
  65.7 0.0 collective-permute-done.14.refs_5_
  65.7 7.8 %collective-permute-done.15.refs_6_ = bf16[512,512]{1,0:T(8,128)(2,1)S(1)} collective-permute-done((bf16[512,512]{1,0:T(8,128)(2,1)S(1)}, bf16[512,512]{1,0:T(8,128)(2,1)S(1)}, u32[]{:S(2)}, u32[]{:S(2)}) %collective-permute-start.15) | collective-permute-done | bytes 524320 | tf_op jit(solution)/shard_map/ppermute | solution.py:460
  73.5 3.5 %attend.10 = bf16[256,768]{1,0:T(8,128)(2,1)S(1)} custom-call(s32[1]{0:T(128)} %bitcast.own_ref.refs_0_, s32[16]{0:T(128)S(1)} %copy-done.2, s32[8,8]{1,0:T(8,128)S(1)} %copy-done.1, bf16[2,6,128,256]{3,2,1,0:T(8,128)(2,1)S(1)} %turn.1.refs_3_, f32[2,6,144,256]{3,2,1,0:T(8,128)S(1)} %attend.9.refs_4_, bf16[512,512]{1,0:T(8,128)(2,1)S(1)} %collective-permute-done.14.refs_5_, ...), custom_call_target="tpu_custom_call" | custom-call | flops 1 | bytes 1 | tf_op jit(solution)/shard_map/attend/pallas_call | solution.py:307
  77.0 0.1 collective-permute-start.16
  77.1 3.8 %attend.11.refs_1_ = bf16[256,768]{1,0:T(8,128)(2,1)S(1)} custom-call(s32[1]{0:T(128)} %bitcast.own_ref.refs_0_, s32[16]{0:T(128)S(1)} %copy-done.2, s32[8,8]{1,0:T(8,128)S(1)} %copy-done.1, bf16[2,6,128,256]{3,2,1,0:T(8,128)(2,1)S(1)} %turn.1.refs_3_, f32[2,6,144,256]{3,2,1,0:T(8,128)S(1)} %attend.9.refs_4_, ...), custom_call_target="tpu_custom_call" | custom-call | flops 1 | bytes 1 | tf_op jit(solution)/shard_map/attend/pallas_call | solution.py:307
  80.9 1.7 %project.4.refs_3_ = f32[128,3072]{1,0:T(8,128)S(1)} custom-call(s32[1]{0:T(128)} %bitcast.own_ref.refs_0_, bf16[256,768]{1,0:T(8,128)(2,1)S(1)} %attend.11.refs_1_, bf16[1536,3072]{1,0:T(8,128)(2,1)S(1)} %fetch.1.refs_3_.refs_2_), custom_call_target="tpu_custom_call" | custom-call | flops 603979776 | bytes 4718592 | tf_op jit(solution)/shard_map/project/pallas_call | solution.py:413
  82.6 0.0 copy-start
  82.6 0.0 copy-start.3
  82.6 0.0 collective-permute-done.16.refs_2_.refs_1_
  82.6 1.7 %project.5 = bf16[128,3072]{1,0:T(8,128)(2,1)S(1)} custom-call(s32[1]{0:T(128)} %bitcast.own_ref.refs_0_, bf16[256,768]{1,0:T(8,128)(2,1)S(1)} %collective-permute-done.16.refs_2_.refs_1_, bf16[1536,3072]{1,0:T(8,128)(2,1)S(1)} %fetch.1.refs_3_.refs_2_, f32[128,3072]{1,0:T(8,128)S(1)} %project.4.refs_3_), custom_call_target="tpu_custom_call" | custom-call | flops 603979776 | bytes 4718592 | tf_op jit(solution)/shard_map/project/pallas_call | solution.py:413
  84.3 0.1 collective-permute-start.17
  84.4 0.0 copy-done
  84.4 0.0 copy-done.3
  84.4 4.0 %project.3 = (f32[128,3072]{1,0:T(8,128)S(1)}, f32[8,3072]{1,0:T(8,128)S(1)}) custom-call(s32[1]{0:T(128)} %bitcast.own_ref.refs_0_, bf16[256,768]{1,0:T(8,128)(2,1)S(1)} %attend.11.refs_1_, bf16[256,768]{1,0:T(8,128)(2,1)S(1)} %collective-permute-done.16.refs_2_.refs_1_, bf16[1536,3072]{1,0:T(8,128)(2,1)S(1)} %fetch.1.refs_3_.refs_2_, s32[8]{0:T(128)S(1)} %copy-done.3, ...), custom_call_target="tpu_custom_call" | custom-call | flops 1207959552 | bytes 9437184 | tf_op jit(solution)/shard_map/project/pallas_call | solution.py:413
  88.4 15.9 %collective-permute-done.17 = bf16[128,3072]{1,0:T(8,128)(2,1)S(1)} collective-permute-done((bf16[128,3072]{1,0:T(8,128)(2,1)S(1)}, bf16[128,3072]{1,0:T(8,128)(2,1)S(1)}, u32[]{:S(2)}, u32[]{:S(2)}) %collective-permute-start.17) | collective-permute-done | bytes 786464 | tf_op jit(solution)/shard_map/ppermute | solution.py:515
  104.3 1.1 %add_convert_fusion = bf16[128,3072]{1,0:T(8,128)(2,1)} fusion(f32[128,3072]{1,0:T(8,128)S(1)} %get-tuple-element.41, bf16[128,3072]{1,0:T(8,128)(2,1)S(1)} %collective-permute-done.17, f32[3072]{0:T(1024)S(1)} %bitcast.2), kind=kLoop, calls=%fused_computation | loop fusion | flops 1572864 | bytes 3158016 | tf_op jit(solution)/shard_map/convert_element_type | solution.py:517
  (8 shorter events, 0.1 us)
Async XLA Ops:
  0.0 3.6 %copy-start.4 = (bf16[128,3072]{1,0:T(8,128)(2,1)S(1)}, bf16[128,3072]{1,0:T(8,128)(2,1)}, u32[]{:S(2)}) copy-start(bf16[128,3072]{1,0:T(8,128)(2,1)} %param.9) | copy-start | bytes 2359300
  1.2 6.0 %collective-permute-start.1 = (bf16[128,512]{1,0:T(8,128)(2,1)S(1)}, bf16[128,512]{1,0:T(8,128)(2,1)S(1)}, u32[]{:S(2)}, u32[]{:S(2)}) collective-permute-start(bf16[128,512]{1,0:T(8,128)(2,1)S(1)} %pad_maximum_fusion.4), channel_id=1, source_target_pairs={{1,0},{0,1},{3,2},{2,3},{5,4},{4,5},{7,6},{6,7},{9,8},{8,9},{11,10... | collective-permute-start | bytes 393224 | tf_op jit(solution)/shard_map/ppermute | solution.py:448
  2.8 5.9 %collective-permute-start.2 = (bf16[128,512]{1,0:T(8,128)(2,1)S(1)}, bf16[128,512]{1,0:T(8,128)(2,1)S(1)}, u32[]{:S(2)}, u32[]{:S(2)}) collective-permute-start(bf16[128,512]{1,0:T(8,128)(2,1)S(1)} %pad_maximum_fusion.5), channel_id=1, source_target_pairs={{3,0},{2,1},{1,2},{0,3},{7,4},{6,5},{5,6},{4,7},{11,8},{10,9},{9,1... | collective-permute-start | bytes 393224 | tf_op jit(solution)/shard_map/ppermute | solution.py:448
  2.9 5.8 %collective-permute-start = (bf16[128,512]{1,0:T(8,128)(2,1)S(1)}, bf16[128,512]{1,0:T(8,128)(2,1)S(1)}, u32[]{:S(2)}, u32[]{:S(2)}) collective-permute-start(bf16[128,512]{1,0:T(8,128)(2,1)S(1)} %pad_maximum_fusion.3), channel_id=1, source_target_pairs={{2,0},{3,1},{0,2},{1,3},{6,4},{7,5},{4,6},{5,7},{10,8},{11,9},{8,1... | collective-permute-start | bytes 393224 | tf_op jit(solution)/shard_map/ppermute | solution.py:448
  8.7 11.6 %collective-permute-start.3 = (bf16[128,1536]{1,0:T(8,128)(2,1)S(1)}, bf16[128,1536]{1,0:T(8,128)(2,1)S(1)}, u32[]{:S(2)}, u32[]{:S(2)}) collective-permute-start(bf16[128,1536]{1,0:T(8,128)(2,1)S(1)} %get-tuple-element.25), channel_id=1, source_target_pairs={{1,0},{0,1},{3,2},{2,3},{5,4},{4,5},{7,6},{6,7},{9,8},{8,9},{11,10... | collective-permute-start | bytes 1179656 | tf_op jit(solution)/shard_map/ppermute | solution.py:448
  9.8 15.0 %collective-permute-start.9 = (bf16[512,512]{1,0:T(8,128)(2,1)S(1)}, bf16[512,512]{1,0:T(8,128)(2,1)S(1)}, u32[]{:S(2)}, u32[]{:S(2)}) collective-permute-start(bf16[512,512]{1,0:T(8,128)(2,1)S(1)} %pad_maximum_fusion.refs_4_), channel_id=1, source_target_pairs={{4,0},{6,2},{0,4},{2,6},{12,8},{14,10},{8,12},{10,14},{20,16},{22,... | collective-permute-start | bytes 1572872 | tf_op jit(solution)/shard_map/ppermute | solution.py:460
  10.3 12.6 %collective-permute-start.7 = (bf16[256,512]{1,0:T(8,128)(2,1)S(1)}, bf16[256,512]{1,0:T(8,128)(2,1)S(1)}, u32[]{:S(2)}, u32[]{:S(2)}) collective-permute-start(bf16[256,512]{1,0:T(8,128)(2,1)S(1)} %pad_maximum_fusion.2), channel_id=1, source_target_pairs={{0,8},{2,10},{4,12},{6,14},{8,0},{10,2},{12,4},{14,6},{16,24},{18,... | collective-permute-start | bytes 786440 | tf_op jit(solution)/shard_map/ppermute | solution.py:454
  10.8 25.4 %collective-permute-start.5 = (bf16[512,512]{1,0:T(8,128)(2,1)S(1)}, bf16[512,512]{1,0:T(8,128)(2,1)S(1)}, u32[]{:S(2)}, u32[]{:S(2)}) collective-permute-start(bf16[512,512]{1,0:T(8,128)(2,1)S(1)} %pad_maximum_fusion.refs_4_), channel_id=1, source_target_pairs={{0,16},{2,18},{4,20},{6,22},{8,24},{10,26},{12,28},{14,30},{16,0},... | collective-permute-start | bytes 1572872 | tf_op jit(solution)/shard_map/ppermute | solution.py:454
  20.3 4.5 %copy-start.1 = (s32[8,8]{1,0:T(8,128)S(1)}, s32[8,8]{1,0:T(8,128)}, u32[]{:S(2)}) copy-start(s32[8,8]{1,0:T(8,128)} %refs_2_.11) | copy-start | bytes 772
  20.3 4.5 %copy-start.2 = (s32[16]{0:T(128)S(1)}, s32[16]{0:T(128)}, u32[]{:S(2)}) copy-start(s32[16]{0:T(128)} %refs_5_.1) | copy-start | bytes 196
  20.3 4.2 %collective-permute-start.4 = (bf16[256,768]{1,0:T(8,128)(2,1)S(1)}, bf16[256,768]{1,0:T(8,128)(2,1)S(1)}, u32[]{:S(2)}, u32[]{:S(2)}) collective-permute-start(bf16[256,768]{1,0:T(8,128)(2,1)S(1)} %other_columns.1), channel_id=1, source_target_pairs={{2,0},{3,1},{0,2},{1,3},{6,4},{7,5},{4,6},{5,7},{10,8},{11,9},{8,1... | collective-permute-start | bytes 1179656 | tf_op jit(solution)/shard_map/ppermute | solution.py:448
  20.4 15.5 %collective-permute-start.6 = (bf16[256,512]{1,0:T(8,128)(2,1)S(1)}, bf16[256,512]{1,0:T(8,128)(2,1)S(1)}, u32[]{:S(2)}, u32[]{:S(2)}) collective-permute-start(bf16[256,512]{1,0:T(8,128)(2,1)S(1)} %pad_maximum_fusion.1), channel_id=1, source_target_pairs={{0,8},{2,10},{4,12},{6,14},{8,0},{10,2},{12,4},{14,6},{16,24},{18,... | collective-permute-start | bytes 786440 | tf_op jit(solution)/shard_map/ppermute | solution.py:454
  23.0 13.0 %collective-permute-start.8 = (bf16[256,512]{1,0:T(8,128)(2,1)S(1)}, bf16[256,512]{1,0:T(8,128)(2,1)S(1)}, u32[]{:S(2)}, u32[]{:S(2)}) collective-permute-start(bf16[256,512]{1,0:T(8,128)(2,1)S(1)} %collective-permute-done.7.refs_5_), channel_id=1, source_target_pairs={{4,0},{6,2},{0,4},{2,6},{12,8},{14,10},{8,12},{10,14},{20,16},{22,... | collective-permute-start | bytes 786440 | tf_op jit(solution)/shard_map/ppermute | solution.py:460
  36.2 18.3 %collective-permute-start.10 = (bf16[512,512]{1,0:T(8,128)(2,1)S(1)}, bf16[512,512]{1,0:T(8,128)(2,1)S(1)}, u32[]{:S(2)}, u32[]{:S(2)}) collective-permute-start(bf16[512,512]{1,0:T(8,128)(2,1)S(1)} %collective-permute-done.5.refs_7_), channel_id=1, source_target_pairs={{8,0},{10,2},{12,4},{14,6},{16,24},{18,26},{20,28},{22,30},{9,1},{... | collective-permute-start | bytes 1572872 | tf_op jit(solution)/shard_map/ppermute | solution.py:454
  40.5 14.8 %collective-permute-start.11 = (bf16[512,512]{1,0:T(8,128)(2,1)S(1)}, bf16[512,512]{1,0:T(8,128)(2,1)S(1)}, u32[]{:S(2)}, u32[]{:S(2)}) collective-permute-start(bf16[512,512]{1,0:T(8,128)(2,1)S(1)} %pad_maximum_fusion.refs_4_), channel_id=1, source_target_pairs={{8,16},{10,18},{12,20},{14,22},{16,8},{18,10},{20,12},{22,14},{9,1... | collective-permute-start | bytes 1572872 | tf_op jit(solution)/shard_map/ppermute | solution.py:454
  44.0 9.3 %collective-permute-start.12 = (bf16[256,512]{1,0:T(8,128)(2,1)S(1)}, bf16[256,512]{1,0:T(8,128)(2,1)S(1)}, u32[]{:S(2)}, u32[]{:S(2)}) collective-permute-start(bf16[256,512]{1,0:T(8,128)(2,1)S(1)} %collective-permute-done.6.refs_6_), channel_id=1, source_target_pairs={{4,0},{6,2},{0,4},{2,6},{12,8},{14,10},{8,12},{10,14},{20,16},{22,... | collective-permute-start | bytes 786440 | tf_op jit(solution)/shard_map/ppermute | solution.py:460
  45.6 19.0 %collective-permute-start.13 = (bf16[512,512]{1,0:T(8,128)(2,1)S(1)}, bf16[512,512]{1,0:T(8,128)(2,1)S(1)}, u32[]{:S(2)}, u32[]{:S(2)}) collective-permute-start(bf16[512,512]{1,0:T(8,128)(2,1)S(1)} %collective-permute-done.5.refs_7_), channel_id=1, source_target_pairs={{4,0},{6,2},{0,4},{2,6},{12,8},{14,10},{8,12},{10,14},{20,16},{22,... | collective-permute-start | bytes 1572872 | tf_op jit(solution)/shard_map/ppermute | solution.py:460
  55.3 10.4 %collective-permute-start.14 = (bf16[512,512]{1,0:T(8,128)(2,1)S(1)}, bf16[512,512]{1,0:T(8,128)(2,1)S(1)}, u32[]{:S(2)}, u32[]{:S(2)}) collective-permute-start(bf16[512,512]{1,0:T(8,128)(2,1)S(1)} %collective-permute-done.10.refs_6_), channel_id=1, source_target_pairs={{4,0},{6,2},{0,4},{2,6},{28,24},{30,26},{24,28},{26,30},{5,1},{7,3... | collective-permute-start | bytes 1572872 | tf_op jit(solution)/shard_map/ppermute | solution.py:460
  56.0 17.5 %collective-permute-start.15 = (bf16[512,512]{1,0:T(8,128)(2,1)S(1)}, bf16[512,512]{1,0:T(8,128)(2,1)S(1)}, u32[]{:S(2)}, u32[]{:S(2)}) collective-permute-start(bf16[512,512]{1,0:T(8,128)(2,1)S(1)} %collective-permute-done.11.refs_7_), channel_id=1, source_target_pairs={{12,8},{14,10},{8,12},{10,14},{20,16},{22,18},{16,20},{18,22},{13,... | collective-permute-start | bytes 1572872 | tf_op jit(solution)/shard_map/ppermute | solution.py:460
  77.0 5.6 %collective-permute-start.16 = (bf16[256,768]{1,0:T(8,128)(2,1)S(1)}, bf16[256,768]{1,0:T(8,128)(2,1)S(1)}, u32[]{:S(2)}, u32[]{:S(2)}) collective-permute-start(bf16[256,768]{1,0:T(8,128)(2,1)S(1)} %attend.10), channel_id=1, source_target_pairs={{2,0},{3,1},{0,2},{1,3},{6,4},{7,5},{4,6},{5,7},{10,8},{11,9},{8,1... | collective-permute-start | bytes 1179656 | tf_op jit(solution)/shard_map/ppermute | solution.py:448
  82.6 1.9 %copy-start = (bf16[128,3072]{1,0:T(8,128)(2,1)S(1)}, bf16[128,3072]{1,0:T(8,128)(2,1)}, u32[]{:S(2)}) copy-start(bf16[128,3072]{1,0:T(8,128)(2,1)} %refs_7_.1) | copy-start | bytes 2359300
  82.6 1.8 %copy-start.3 = (s32[8]{0:T(128)S(1)}, s32[8]{0:T(128)}, u32[]{:S(2)}) copy-start(s32[8]{0:T(128)} %refs_4_.1) | copy-start | bytes 100
  84.3 20.0 %collective-permute-start.17 = (bf16[128,3072]{1,0:T(8,128)(2,1)S(1)}, bf16[128,3072]{1,0:T(8,128)(2,1)S(1)}, u32[]{:S(2)}, u32[]{:S(2)}) collective-permute-start(bf16[128,3072]{1,0:T(8,128)(2,1)S(1)} %project.5), channel_id=1, source_target_pairs={{0,1},{1,0},{2,3},{3,2},{4,5},{5,4},{6,7},{7,6},{8,9},{9,8},{10,11... | collective-permute-start | bytes 2359304 | tf_op jit(solution)/shard_map/ppermute | solution.py:515

commit v2 on v1

--- a/solution.py
+++ b/solution.py
@@ -13,6 +13,7 @@
 HEAD_DIM = 128
 GROUP = Q_HEADS // KV_HEADS
 CORES = 2
+UNITS = 2
 NEG = -1e30
 SCALE = 1.4426950408889634 * HEAD_DIM ** -0.5
 STAT = 8
@@ -28,13 +29,15 @@
     return chips // inner, inner
 
 
-def attend_kernel(place, n_items, parts, mine, rows, tok, first, last, refs):
-    own_ref, map_ref, mask_ref, qt = refs[:4]
+def attend_kernel(place, n_items, parts, half, rows, tok, first, last, refs):
+    own_ref, map_ref, mask_ref, q_ref = refs[:4]
+    mixed = half is not None
+    tiles = 1 if mixed else parts
     state_in = None if first else refs[4]
-    items = refs[4 if first else 5 : -10]
-    out_ref = refs[-10]
-    st_s, kv_s, vt_s, list_s, land_s, full_s, count_s, top_s, sems = refs[-9:]
-    st = st_s if last else out_ref
+    st_s, qt_s, kv_s, vt_s, list_s, land_s, seen_s, full_s, count_s, top_s, sems = refs[-11:]
+    outs = 2 if mixed else 1
+    items, outs = refs[4 if first else 5 : -11 - outs], refs[-11 - outs : -11]
+    st, qt = st_s if last else outs[0], qt_s if mixed else q_ref
     heads = qt.shape[1]
     kv_heads = heads // GROUP
     kvw = kv_heads * HEAD_DIM
@@ -52,7 +55,7 @@
         ]
 
     seg_q = [map_ref[place.query(own, j)] for j in range(parts)]
-    counts = [jnp.int32(0)] * parts
+    counts = [jnp.int32(0)] * tiles
     landed = jnp.int32(0)
     for i in range(n_items):
         for kp in range(parts):
@@ -60,13 +63,18 @@
             valid, src = place.source(own, i, kp)
             seg_k = map_ref[src]
             any_seen = jnp.int32(0)
-            for qp in mine:
+            for qp in range(parts):
                 seen = (mask_ref[seg_q[qp], seg_k] > 0).astype(jnp.int32)
                 if valid is not None:
                     seen = seen * valid.astype(jnp.int32)
-                list_s[qp, counts[qp]] = ik
-                counts[qp] = counts[qp] + seen
+                seen_s[qp, ik] = seen
                 any_seen = jnp.maximum(any_seen, seen)
+                if not mixed:
+                    list_s[qp, counts[qp]] = ik
+                    counts[qp] = counts[qp] + seen
+            if mixed:
+                list_s[0, counts[0]] = ik
+                counts[0] = counts[0] + any_seen
             land_s[landed] = ik
             landed = landed + any_seen
 
@@ -93,53 +101,91 @@
         single = 2 * t + 1 >= full_s[qp]
         i0 = list_s[qp, 2 * t]
         i1 = list_s[qp, jnp.where(single, 2 * t, 2 * t + 1)]
-        return i0, i1, jnp.where(single, jnp.float32(NEG), jnp.float32(0.0))
-
-    def scores(qp, h, i0, i1):
-        lanes = slice((h // GROUP) * HEAD_DIM, (h // GROUP + 1) * HEAD_DIM)
-        k = jnp.concatenate([kv_s[i0, :, lanes], kv_s[i1, :, lanes]], axis=0)
-        s = jnp.dot(k, qt[qp, h], preferred_element_type=jnp.float32)
-        return s.reshape(2, tok // STAT, STAT, rows) * SCALE
-
-    def product(h, i0, i1, s, ref0, ref1):
-        p0 = jnp.exp2(s[0] - ref0[None]).reshape(tok, rows).astype(jnp.bfloat16)
-        p1 = jnp.exp2(s[1] - ref1[None]).reshape(tok, rows).astype(jnp.bfloat16)
-        vt = jnp.concatenate([vt_s[i0, h // GROUP], vt_s[i1, h // GROUP]], axis=1)
-        pv = jnp.dot(vt, jnp.concatenate([p0, p1], axis=0), preferred_element_type=jnp.float32)
-        return pv[sums]
-
-    def slow(qp, t):
+        bias = [jnp.float32(0.0), jnp.where(single, jnp.float32(NEG), jnp.float32(0.0))]
+        if mixed:
+            left = lax.broadcasted_iota(jnp.int32, (STAT, rows), 1) < rows // 2
+            for j, i in enumerate((i0, i1)):
+                hidden = [jnp.where(seen_s[part, i] > 0, jnp.float32(0.0), jnp.float32(NEG)) for part in range(2)]
+                bias[j] = bias[j] + jnp.where(left, hidden[0], hidden[1])
+        return i0, i1, bias
+
+    def operands(kh, i0, i1):
+        lanes = slice(kh * HEAD_DIM, (kh + 1) * HEAD_DIM)
+        return (
+            [jnp.concatenate([kv_s[i, :, lanes]] * 2, axis=1) for i in (i0, i1)],
+            [vt_s[i, kh] for i in (i0, i1)],
+        )
+
+    def slow(units, qp, t):
         i0, i1, bias = blocks(qp, t)
         for h in range(heads):
-            s = scores(qp, h, i0, i1)
+            kh = h // GROUP
+            unit = kh % UNITS
+            s0_acc, s1_acc, pv_acc = units[unit]
+            keys, values = operands(kh, i0, i1)
+            pltpu.matmul_push_rhs(qt[qp, h], 0, unit)
+            pltpu.matmul_acc_lhs(s0_acc, keys[0], 0)
+            pltpu.matmul_acc_lhs(s1_acc, keys[1])
+            s = [pltpu.matmul_pop(acc).reshape(-1, STAT, rows) for acc in (s0_acc, s1_acc)]
             before = st[qp, h, point]
-            top = jnp.maximum(jnp.max(s[0], axis=0), jnp.max(s[1], axis=0) + bias)
+            top = jnp.maximum(jnp.max(s[0], axis=0) + bias[0], jnp.max(s[1], axis=0) + bias[1])
             now = jnp.maximum(before, jnp.max(top, axis=0, keepdims=True))
-            pv = product(h, i0, i1, s, now, now - bias)
+            for x, ref, value in zip(s, (now - bias[0], now - bias[1]), values):
+                p = jnp.exp2(x - ref[None]).reshape(tok, rows).astype(jnp.bfloat16)
+                pltpu.matmul_push_rhs(p, 1, unit)
+                pltpu.matmul_acc_lhs(pv_acc, value, 1)
             kept = st[qp, h, sums].reshape(-1, STAT, rows) * jnp.exp2(before - now)[None]
-            st[qp, h, sums] = kept.reshape(-1, rows) + pv
+            st[qp, h, sums] = kept.reshape(-1, rows) + pltpu.matmul_pop(pv_acc)[sums]
             st[qp, h, point] = now
 
-    def fast(qp, t):
+    def fast(units, qp, t):
         i0, i1, bias = blocks(qp, t)
-        old = [st[qp, h] for h in range(heads)]
-        new = []
+        keys, values = zip(*[operands(kh, i0, i1) for kh in range(kv_heads)])
+
+        def begin(kh, g):
+            unit = units[kh % len(units)]
+            pltpu.matmul_push_rhs(qt[qp, kh * GROUP + g], 0, kh % len(units))
+            pltpu.matmul_acc_lhs(unit[0], keys[kh][0], 0)
+            pltpu.matmul_acc_lhs(unit[1], keys[kh][1])
+
+        def weights_of(kh, g, j):
+            s = pltpu.matmul_pop(units[kh % len(units)][j]).reshape(-1, STAT, rows)
+            ref = st[qp, kh * GROUP + g, point] - bias[j]
+            return jnp.exp2(s - ref[None]).reshape(tok, rows).astype(jnp.bfloat16)
+
+        for first_kh in range(0, kv_heads, len(units)):
+            together = range(first_kh, min(first_kh + len(units), kv_heads))
+            for kh in together:
+                begin(kh, 0)
+            for g in range(GROUP):
+                p = {(kh, j): weights_of(kh, g, j) for j in range(2) for kh in together}
+                if g + 1 < GROUP:
+                    for kh in together:
+                        begin(kh, g + 1)
+                for j in range(2):
+                    for kh in together:
+                        pltpu.matmul_push_rhs(p[kh, j], 1, kh % len(units))
+                        pltpu.matmul_acc_lhs(units[kh % len(units)][2], values[kh][j], 1)
+                for kh in together:
+                    h = kh * GROUP + g
+                    st[qp, h, sums] = st[qp, h, sums] + pltpu.matmul_pop(units[kh % len(units)][2])[sums]
+
+    columns_of = slice(half * rows // 2, (half + 1) * rows // 2) if mixed else slice(0, rows)
+    if mixed:
         for h in range(heads):
-            ref = old[h][point]
-            new.append(old[h][sums] + product(h, i0, i1, scores(qp, h, i0, i1), ref, ref - bias))
-        for h in range(heads):
-            st[qp, h, sums] = new[h]
-
-    for qp in mine:
+            qt_s[0, h] = jnp.concatenate([q_ref[part, h, :, columns_of] for part in range(2)], axis=1)
+    for qp in range(tiles):
         full_s[qp] = counts[qp]
         count_s[qp] = (counts[qp] + 1) // 2
 
     def attempt(again, carry):
         @pl.when(jnp.logical_or(again == 0, top_s[0] > 0))
         def _():
-            for qp in mine:
+            for qp in range(tiles):
                 for h in range(heads):
-                    if first:
+                    if mixed:
+                        st[0, h] = jnp.concatenate([state_in[part, h, :, columns_of] for part in range(2)], axis=1)
+                    elif first:
                         st[qp, h, sums] = jnp.zeros((HEAD_DIM + STAT, rows), jnp.float32)
                         st[qp, h, point] = jnp.full((STAT, rows), NEG, jnp.float32)
                     else:
@@ -149,21 +195,30 @@
                 pairs = count_s[qp]
                 switch = jnp.where(again > 0, pairs, 1 if first else 0)
 
-                def one_slow(t, carry):
-                    slow(qp, t)
-                    return carry
-
-                def one_fast(t, carry):
-                    fast(qp, t)
-                    return carry
-
-                lax.fori_loop(0, switch, one_slow, 0)
-                lax.fori_loop(switch, pairs, one_fast, 0)
+                def both(*accs):
+                    units = [accs[3 * unit : 3 * unit + 3] for unit in range(UNITS)]
+
+                    def one_slow(t, carry):
+                        slow(units, qp, t)
+                        return carry
+
+                    def one_fast(t, carry):
+                        fast(units, qp, t)
+                        return carry
+
+                    lax.fori_loop(0, switch, one_slow, 0)
+                    lax.fori_loop(switch, pairs, one_fast, 0)
+
+                accumulators = []
+                for unit in range(UNITS):
+                    accumulators += [pltpu.ACC(unit)((tok, rows), jnp.float32)] * 2
+                    accumulators.append(pltpu.ACC(unit)((HEAD_DIM + ONES, rows), jnp.float32))
+                pl.run_scoped(both, *accumulators)
                 return carry
 
-            lax.fori_loop(mine[0], mine[-1] + 1, one_part, 0)
+            lax.fori_loop(0, tiles, one_part, 0)
             top = jnp.zeros((STAT, rows), jnp.float32)
-            for qp in mine:
+            for qp in range(tiles):
                 for h in range(heads):
                     top = jnp.maximum(top, jnp.where(st[qp, h, weights] < LARGE, 0.0, 1.0))
             top_s[0] = (jnp.max(top) > 0.0).astype(jnp.int32)
@@ -173,36 +228,37 @@
     top_s[0] = 0
     lax.fori_loop(0, 2, attempt, 0)
     if last:
-        for j, qp in enumerate(mine):
+        for qp in range(tiles):
             for h in range(heads):
+                lanes = slice(h * HEAD_DIM, (h + 1) * HEAD_DIM)
                 inv = 1.0 / st[qp, h, weights]
                 att = st[qp, h, :HEAD_DIM].reshape(-1, STAT, rows) * inv[None]
-                out_ref[j * rows : (j + 1) * rows, h * HEAD_DIM : (h + 1) * HEAD_DIM] = (
-                    att.reshape(HEAD_DIM, rows).T.astype(jnp.bfloat16)
-                )
+                att = att.reshape(HEAD_DIM, rows).T.astype(jnp.bfloat16)
+                if mixed:
+                    outs[0][:, lanes] = att[: rows // 2]
+                    outs[1][:, lanes] = att[rows // 2 :]
+                else:
+                    outs[0][qp * rows : (qp + 1) * rows, lanes] = att
 
 
 class GridPlace:
-    def __init__(self, metas, n_a, n_b):
-        self.metas, self.n_a, self.n_b = metas, n_a, n_b
+    def __init__(self, metas, n_a, n_b, tok):
+        self.metas, self.n_a, self.n_b, self.tok = metas, n_a, n_b, tok
 
     def query(self, own, part):
         return (own // CORES) * CORES + (own % CORES + part) % CORES
 
     def source(self, own, i, part):
-        flip, db, only, _ = self.metas[i]
+        flip, db, _ = self.metas[i]
         a, b, c = own // (CORES * self.n_b), (own // CORES) % self.n_b, own % CORES
-        valid = None
-        if len(only) < self.n_a:
-            valid = functools.reduce(jnp.logical_or, [a == one for one in only])
-        return valid, ((a ^ flip) * self.n_b + (b + db) % self.n_b) * CORES + (c + part) % CORES
+        return None, ((a ^ flip) * self.n_b + (b + db) % self.n_b) * CORES + (c + part) % CORES
 
     def refs(self, items, i, part):
-        first = sum(len(meta[3]) for meta in self.metas[:i])
+        first = sum(len(meta[2]) for meta in self.metas[:i])
         out = []
-        for ref, halves in zip(items[first:], self.metas[i][3]):
-            rows = ref.shape[0] // (CORES * halves)
-            out += [ref.at[pl.ds((half * CORES + part) * rows, rows)] for half in range(halves)]
+        for ref, (halves, base) in zip(items[first:], self.metas[i][2]):
+            rows = self.tok // 2
+            out += [ref.at[pl.ds(base + (half * CORES + part) * rows, rows)] for half in range(halves)]
         return out
 
 
@@ -239,6 +295,55 @@
         cost_estimate=LITTLE,
         name="other_columns",
     )(own, *pieces)
+
+
+def moved(kernel, args, shapes, name):
+    vmem = pl.BlockSpec(memory_space=pltpu.VMEM)
+    return pl.pallas_call(
+        kernel,
+        out_shape=[jax.ShapeDtypeStruct(shape, jnp.bfloat16) for shape in shapes],
+        in_specs=[pl.BlockSpec(memory_space=pltpu.SMEM)] + [vmem] * (len(args) - 1),
+        out_specs=[vmem] * len(shapes),
+        compiler_params=pltpu.CompilerParams(vmem_limit_bytes=VMEM_LIMIT),
+        cost_estimate=LITTLE,
+        name=name,
+    )(*args)
+
+
+def joined(own, above, below):
+    rows, width = above.shape
+
+    def kernel(own_ref, above_ref, below_ref, out_ref):
+        out_ref[:rows] = above_ref[...]
+        out_ref[rows:] = below_ref[...]
+
+    return moved(kernel, (own, above, below), [(2 * rows, width)], "joined")[0]
+
+
+def lower_half(own, x):
+    rows, width = x.shape
+
+    def kernel(own_ref, x_ref, out_ref):
+        out_ref[...] = x_ref[rows // 2 :]
+
+    return moved(kernel, (own, x), [(rows // 2, width)], "lower_half")[0]
+
+
+def picked(own, at_ends, at_middle, n_a, n_b):
+    rows, width = at_ends.shape
+
+    def kernel(own_ref, ends_ref, middle_ref, whole_ref, half_ref):
+        a = own_ref[0] // (CORES * n_b)
+        at_end = jnp.logical_or(a == 0, a == n_a - 1)
+
+        def take(ref):
+            whole_ref[...] = ref[...]
+            half_ref[...] = ref[: rows // 2]
+
+        pl.when(at_end)(lambda: take(ends_ref))
+        pl.when(jnp.logical_not(at_end))(lambda: take(middle_ref))
+
+    return moved(kernel, (own, at_ends, at_middle), [(rows, width), (rows // 2, width)], "picked")
 
 
 def turn(own, parts):
@@ -260,11 +365,14 @@
                     if ref.shape[1] > heads * HEAD_DIM:
                         first = pl.multiple_of(begin + first, HEAD_DIM)
                     turned.append(ref[:, pl.ds(first, HEAD_DIM)].astype(jnp.float32).T)
-                refs[-1][qp, h] = jnp.concatenate(turned, axis=1).astype(jnp.bfloat16)
+                scaled = jnp.concatenate(turned, axis=1) * SCALE
+                high = scaled.astype(jnp.bfloat16)
+                refs[-1][qp, h, :HEAD_DIM] = high
+                refs[-1][qp, h, HEAD_DIM:] = (scaled - high.astype(jnp.float32)).astype(jnp.bfloat16)
 
     return pl.pallas_call(
         kernel,
-        out_shape=pltpu.VMEM((len(parts), heads, HEAD_DIM, rows), jnp.bfloat16),
+        out_shape=pltpu.VMEM((len(parts), heads, 2 * HEAD_DIM, rows), jnp.bfloat16),
         in_specs=[pl.BlockSpec(memory_space=pltpu.SMEM)] + [vmem] * len(pieces),
         out_specs=vmem,
         compiler_params=pltpu.CompilerParams(vmem_limit_bytes=VMEM_LIMIT),
@@ -273,8 +381,7 @@
     )(own, *pieces)
 
 
-def attend(scalars, q, state, arrays, place, n_items, parts, tok, last, mine=None):
-    mine = tuple(range(parts)) if mine is None else mine
+def attend(scalars, q, state, arrays, place, n_items, parts, tok, last, half=None):
     first = state is None
     heads, rows = q.shape[1], q.shape[3]
     width = arrays[0].shape[1]
@@ -284,25 +391,30 @@
     specs = [smem] * 3 + [vmem] + ([] if first else [vmem])
     specs += [pl.BlockSpec(memory_space=pl.ANY)] * len(arrays)
     shape = (parts, heads, HEAD_DIM + 2 * STAT, rows)
+    tile_shape = shape if half is None else (1,) + shape[1:]
     blocks = n_items * parts
     scratch = [
-        pltpu.VMEM(shape if last else (STAT, HEAD_DIM), jnp.float32),
+        pltpu.VMEM(tile_shape if last else (STAT, HEAD_DIM), jnp.float32),
+        pltpu.VMEM((1,) + q.shape[1:] if half is not None else (ONES, HEAD_DIM), jnp.bfloat16),
         pltpu.VMEM((blocks, tok, width), jnp.bfloat16),
         pltpu.VMEM((blocks, heads // GROUP, HEAD_DIM + ONES, tok), jnp.bfloat16),
         pltpu.SMEM((parts, blocks + 1), jnp.int32),
         pltpu.SMEM((blocks + 1,), jnp.int32),
+        pltpu.SMEM((parts, blocks), jnp.int32),
         pltpu.SMEM((parts,), jnp.int32),
         pltpu.SMEM((parts,), jnp.int32),
         pltpu.SMEM((1,), jnp.int32),
         pltpu.SemaphoreType.DMA((blocks, 2)),
     ]
     if last:
-        out_shape = [jax.ShapeDtypeStruct((len(mine) * rows, heads * HEAD_DIM), jnp.bfloat16)]
+        out_shape = [jax.ShapeDtypeStruct((parts * rows, heads * HEAD_DIM), jnp.bfloat16)]
+        if half is not None:
+            out_shape = [jax.ShapeDtypeStruct((rows // 2, heads * HEAD_DIM), jnp.bfloat16)] * 2
     else:
         out_shape = [pltpu.VMEM(shape, jnp.float32)]
 
     def kernel(*refs):
-        attend_kernel(place, n_items, parts, mine, rows, tok, first, last, refs)
+        attend_kernel(place, n_items, parts, half, rows, tok, first, last, refs)
 
     return pl.pallas_call(
         kernel,
@@ -459,60 +571,72 @@
         ]
         return lax.ppermute(piece, "seq", pairs)
 
-    def stage(state, q, waiting, last=False, mine=None):
+    def stage(state, q, waiting, last=False, half=None):
         return attend(
-            scalars, q, state, [x for w, _ in waiting for x in w], GridPlace([m for _, m in waiting], n_a, n_b),
-            len(waiting), CORES, tok, last, mine,
+            scalars, q, state, [x for w, _ in waiting for x in w], GridPlace([m for _, m in waiting], n_a, n_b, tok),
+            len(waiting), CORES, tok, last, half,
         )
 
     def kv_for(dx, dc):
         j = (x ^ dx) * CORES + (c ^ dc)
         return jnp.concatenate([columns(key_rows, j, kvw), columns(value_rows, j, kvw)], axis=1)
 
-    ends, middle, chips = [0, 3], [1, 2], list(range(n_a))
+    chips = list(range(n_a))
     order = [(0, 0), (1, 0), (0, 1), (1, 1)]
     pieces = {d: kv_for(*d) if sum(d) == 0 else swapped(kv_for(*d), *d) for d in order}
     early = jnp.concatenate([pieces[0, 0], pieces[0, 1]], axis=0)
     later = jnp.concatenate([pieces[1, 0], pieces[1, 1]], axis=0)
-    next_early = along_a(early, [(a, a ^ 1) for a in chips])
     block = jnp.concatenate([early, later], axis=0)
     qw = query_rows.shape[1] // 2
     q_own, q_other = columns(query_rows, x, qw), columns(query_rows, 1 - x, qw)
-    block, later, out_weight, q_own, q_other = lax.optimization_barrier(
-        (block, later, out_weight, q_own, q_other)
+    block, early, later, out_weight, q_own, q_other = lax.optimization_barrier(
+        (block, early, later, out_weight, q_own, q_other)
     )
+    by_one, by_two = [(a, a ^ 1) for a in chips], [(a, a ^ 2) for a in chips]
     beside = beside_of(block, chips)
-    far = along_a(block, [(a, a ^ 2) for a in chips])
-    next_later = along_a(later, [(a, a ^ 1) for a in chips])
+    next_early, far_early = along_a(early, by_one), along_a(early, by_two)
     q_came = swapped(q_other, 1, 0)
     weight = fetch(out_weight)
-    q_came, weight = lax.optimization_barrier((q_came, weight))
+    beside, next_early, far_early, later, q_came, weight = lax.optimization_barrier(
+        (beside, next_early, far_early, later, q_came, weight)
+    )
+    beside_early = beside_of(joined(own, next_early, far_early), chips)
+    next_later, far_later = along_a(later, by_one), along_a(later, by_two)
     q_core = swapped(other_columns(own, [q_own, q_came]), 0, 1)
     q = turn(own, [[q_own, q_came], [q_core]])
-    beside_early = beside_of(next_early, chips)
-    (state,) = stage(None, q, [([block], (0, 0, chips, [2])), ([beside], (0, 1, chips, [2]))])
-    next_later, beside_early, state = lax.optimization_barrier((next_later, beside_early, state))
-    beside_later = beside_of(next_later, chips)
-    far, again, state = lax.optimization_barrier((far, block, state))
-    to_ends = along_a(far, [(1, 0), (2, 3)])
-    beside_far = beside_of(far, chips)
+    whole, halves = [(2, 0)], [(1, 0), (1, 0)]
+    (state,) = stage(None, q, [([block], (0, 0, whole)), ([beside], (0, 1, whole))])
+    next_later, far_later, beside_early, again, state = lax.optimization_barrier(
+        (next_later, far_later, beside_early, block, state)
+    )
+    beside_later = beside_of(joined(own, next_later, far_later), chips)
+    to_ends = along_a(joined(own, far_early, far_later), [(1, 0), (2, 3)])
     to_middle = along_a(again, [(1, 2), (2, 1)])
-    (state,) = stage(state, q, [([next_early, next_later], (1, 0, chips, [1, 1])), ([far], (2, 0, chips, [2]))])
-    (state,) = stage(state, q, [([beside_early, beside_later], (1, 1, chips, [1, 1]))])
-    to_ends, to_middle, state = lax.optimization_barrier((to_ends, to_middle, state))
+    (state,) = stage(
+        state, q, [([next_early, next_later], (1, 0, halves)), ([far_early, far_later], (2, 0, halves))]
+    )
+    to_ends, to_middle, beside_later, state = lax.optimization_barrier((to_ends, to_middle, beside_later, state))
+    last, last_upper = picked(own, to_ends, to_middle, n_a, n_b)
     beside_last = [
-        ([beside_of(to_ends, ends)], (3, 1, ends, [2])),
-        ([beside_of(to_middle, middle)], (3, 1, middle, [2])),
+        ([beside_of(last_upper, chips), along_a(lower_half(own, beside_later), by_one)], (3, 1, halves)),
     ]
-    last = [([to_ends], (3, 0, ends, [2])), ([to_middle], (3, 0, middle, [2]))]
-    (state,) = stage(state, q, [([beside_far], (2, 1, chips, [2]))] + last)
-    (sent,) = stage(state, q, beside_last, True, (1,))
+    relayed = [beside_early, beside_later]
+    (state,) = stage(
+        state, q,
+        [
+            (relayed, (1, 1, halves)),
+            (relayed, (2, 1, [(1, tok), (1, tok)])),
+            ([last], (3, 0, whole)),
+        ],
+    )
+    kept, sent = stage(state, q, beside_last, True, 1)
     came = swapped(sent, 0, 1)
-    state, sent = lax.optimization_barrier((state, sent))
-    (kept,) = stage(state, q, beside_last, True, (0,))
-    (begun,) = project(own, [(kept, 0, rows)], weight, rows)
-    (theirs,) = project(own, [(came, 1, rows)], weight, rows, partial=begun)
+    (begun,) = project(own, [(kept, 0, 0)], weight, rows)
+    (theirs,) = project(own, [(came, 1, 0)], weight, rows, partial=begun)
     came_back = lax.ppermute(theirs, "head", [(0, 1), (1, 0)])
+    state, theirs = lax.optimization_barrier((state, theirs))
+    kept, sent = stage(state, q, beside_last, True, 0)
+    came = swapped(sent, 0, 1)
     base, gate = project(own, [(kept, 0, 0), (came, 1, 0)], weight, rows, ending=ending)
     return (base + gate[:1] * came_back.astype(jnp.float32)).astype(jnp.bfloat16)
 

time: 106 us -> 103 us (0.972)
  the two profiles are of different devices: /device:TPU:12 before, /device:TPU:0 now
where the time goes in v2:
time: 103 us
  Pallas kernels  41.2 us (40%)
  waiting for transfers between devices  35.1 us (34%)
  starting transfers between devices  23.5 us (23%)
  local copies, waits for them, and re-layouts  1.26 us (1%)
  other arithmetic  1.21 us (1%)
    pallas_call x5, Pallas kernels, attend(): pl.pallas_call(kernel, out_shape=out_shape, in_specs=specs, out_specs=[vm...  29.5 us
    ppermute x7, waiting for transfers between devices, along_a(): return lax.ppermute(piece, 'seq', pairs)  16.6 us
    ppermute x7, starting transfers between devices, along_a(): return lax.ppermute(piece, 'seq', pairs)  13.9 us
    ppermute x1, waiting for transfers between devices, paired(): came_back = lax.ppermute(theirs, 'head', [(0, 1), (1, 0)])  10.6 us
    pallas_call x3, Pallas kernels, project(): pl.pallas_call(kernel, out_shape=out_shape, in_specs=specs, out_specs=[vm...  7.33 us
    ppermute x7, waiting for transfers between devices, swapped(): return lax.ppermute(piece, ('seq', 'head'), pairs)  6.84 us
    ppermute x7, starting transfers between devices, swapped(): return lax.ppermute(piece, ('seq', 'head'), pairs)  4.69 us
    ppermute x4, starting transfers between devices, beside_of(): return lax.ppermute(piece, 'seq', pairs)  4.24 us
  transfers between devices with their start and end apart: 19, of which 10 were waited for; matrix products, arithmetic and copies ran while one was open for 0% of the time, Pallas kernels for 35%

profile of v2, /device:TPU:0, one launch (start us, length us, event | category | flops | bytes accessed | tf_op | source)
XLA Modules:
  0.0 102.5 jit_solution(7318407276133123791)
XLA Ops:
  0.0 0.0 copy-start.4
  0.0 1.2 %constant_dynamic-slice_fusion.8 = (bf16[128,256]{1,0:T(8,128)(2,1)S(1)}, bf16[128,256]{1,0:T(8,128)(2,1)S(1)}, bf16[128,256]{1,0:T(8,128)(2,1)S(1)}, bf16[128,2...) fusion(bf16[128,1024]{1,0:T(8,128)(2,1)} %param.11, ...), kind=kLoop, calls=%fused_computation.15 | loop fusion | bytes 1048592 | tf_op jit(solution)/shard_map/dynamic_slice | solution.py:540
  1.2 3.0 %collective-permute-start.1 = (bf16[128,512]{1,0:T(8,128)(2,1)S(1)}, bf16[128,512]{1,0:T(8,128)(2,1)S(1)}, u32[]{:S(2)}, u32[]{:S(2)}) collective-permute-start(bf16[128,512]{1,0:T(8,128)(2,1)S(1)} %pad_maximum_fusion.4), channel_id=1, source_target_pairs={{1,0},{0,1},{3,2},{2,3},{5,4},{4,5},{7,6},{6,7},{9,8},{8,9},{11,10... | collective-permute-start | bytes 393224 | tf_op jit(solution)/shard_map/ppermute | solution.py:560
  4.2 0.1 collective-permute-start.2
  4.3 0.2 collective-permute-start
  4.5 0.0 copy-done.4
  4.5 0.1 constant_dynamic-slice_fusion
  4.6 3.6 %collective-permute-done.1 = bf16[128,512]{1,0:T(8,128)(2,1)S(1)} collective-permute-done((bf16[128,512]{1,0:T(8,128)(2,1)S(1)}, bf16[128,512]{1,0:T(8,128)(2,1)S(1)}, u32[]{:S(2)}, u32[]{:S(2)}) %collective-permute-start.1) | collective-permute-done | bytes 131104 | tf_op jit(solution)/shard_map/ppermute | solution.py:560
  8.1 2.0 %collective-permute-done.2 = bf16[128,512]{1,0:T(8,128)(2,1)S(1)} collective-permute-done((bf16[128,512]{1,0:T(8,128)(2,1)S(1)}, bf16[128,512]{1,0:T(8,128)(2,1)S(1)}, u32[]{:S(2)}, u32[]{:S(2)}) %collective-permute-start.2) | collective-permute-done | bytes 131104 | tf_op jit(solution)/shard_map/ppermute | solution.py:560
  10.2 0.0 collective-permute-done
  10.2 1.5 %collective-permute-start.3 = (bf16[512,512]{1,0:T(8,128)(2,1)S(1)}, bf16[512,512]{1,0:T(8,128)(2,1)S(1)}, u32[]{:S(2)}, u32[]{:S(2)}) collective-permute-start(bf16[512,512]{1,0:T(8,128)(2,1)S(1)} %pad_maximum_fusion.refs_4_), channel_id=1, source_target_pairs={{4,0},{6,2},{0,4},{2,6},{12,8},{14,10},{8,12},{10,14},{20,16},{22,... | collective-permute-start | bytes 1572872 | tf_op jit(solution)/shard_map/ppermute | solution.py:572
  11.8 1.0 collective-permute-start.6
  12.8 1.6 %collective-permute-start.4 = (bf16[256,512]{1,0:T(8,128)(2,1)S(1)}, bf16[256,512]{1,0:T(8,128)(2,1)S(1)}, u32[]{:S(2)}, u32[]{:S(2)}) collective-permute-start(bf16[256,512]{1,0:T(8,128)(2,1)S(1)} %pad_maximum_fusion.1), channel_id=1, source_target_pairs={{0,8},{2,10},{4,12},{6,14},{8,0},{10,2},{12,4},{14,6},{16,24},{18,... | collective-permute-start | bytes 786440 | tf_op jit(solution)/shard_map/ppermute | solution.py:566
  14.4 2.6 %collective-permute-start.5 = (bf16[256,512]{1,0:T(8,128)(2,1)S(1)}, bf16[256,512]{1,0:T(8,128)(2,1)S(1)}, u32[]{:S(2)}, u32[]{:S(2)}) collective-permute-start(bf16[256,512]{1,0:T(8,128)(2,1)S(1)} %pad_maximum_fusion.1), channel_id=1, source_target_pairs={{0,16},{2,18},{4,20},{6,22},{8,24},{10,26},{12,28},{14,30},{16,0},... | collective-permute-start | bytes 786440 | tf_op jit(solution)/shard_map/ppermute | solution.py:566
  17.0 3.8 %fetch.1.refs_2_.refs_3_ = bf16[1536,3072]{1,0:T(8,128)(2,1)S(1)} custom-call(bf16[1536,3072]{1,0:T(8,128)(2,1)} %weight_ref), custom_call_target="tpu_custom_call" | custom-call | flops 1 | bytes 1 | tf_op jit(solution)/shard_map/fetch/pallas_call | solution.py:451
  20.8 6.2 %collective-permute-done.4.above_ref.refs_5_ = bf16[256,512]{1,0:T(8,128)(2,1)S(1)} collective-permute-done((bf16[256,512]{1,0:T(8,128)(2,1)S(1)}, bf16[256,512]{1,0:T(8,128)(2,1)S(1)}, u32[]{:S(2)}, u32[]{:S(2)}) %collective-permute-start.4) | collective-permute-done | bytes 262176 | tf_op jit(solution)/shard_map/ppermute | solution.py:566
  26.9 2.4 %collective-permute-done.5.below_ref.above_ref.refs_7_ = bf16[256,512]{1,0:T(8,128)(2,1)S(1)} collective-permute-done((bf16[256,512]{1,0:T(8,128)(2,1)S(1)}, bf16[256,512]{1,0:T(8,128)(2,1)S(1)}, u32[]{:S(2)}, u32[]{:S(2)}) %collective-permute-start.5) | collective-permute-done | bytes 262176 | tf_op jit(solution)/shard_map/ppermute | solution.py:566
  29.3 0.0 collective-permute-done.6.refs_1_
  29.3 0.0 collective-permute-done.3.refs_5_
  29.3 0.6 collective-permute-start.10
  29.9 0.0 copy-start.1
  29.9 0.0 copy-start.2
  30.0 0.1 collective-permute-start.7
  30.0 0.5 collective-permute-start.8
  30.6 2.6 %collective-permute-start.9 = (bf16[256,512]{1,0:T(8,128)(2,1)S(1)}, bf16[256,512]{1,0:T(8,128)(2,1)S(1)}, u32[]{:S(2)}, u32[]{:S(2)}) collective-permute-start(bf16[256,512]{1,0:T(8,128)(2,1)S(1)} %pad_maximum_fusion.2), channel_id=1, source_target_pairs={{0,16},{2,18},{4,20},{6,22},{8,24},{10,26},{12,28},{14,30},{16,0},... | collective-permute-start | bytes 786440 | tf_op jit(solution)/shard_map/ppermute | solution.py:566
  33.1 0.0 collective-permute-done.7.refs_2_
  33.1 0.4 turn.1.refs_3_
  33.5 0.0 copy-done.1
  33.6 0.0 copy-done.2
  33.6 7.0 %attend.5.refs_4_ = f32[2,6,144,256]{3,2,1,0:T(8,128)S(1)} custom-call(s32[1]{0:T(128)} %bitcast.own_ref.refs_0_, s32[16]{0:T(128)S(1)} %copy-done.2, s32[8,8]{1,0:T(8,128)S(1)} %copy-done.1, bf16[2,6,256,256]{3,2,1,0:T(8,128)(2,1)S(1)} %turn.1.refs_3_, bf16[512,512]{1,0:T(8,128)(2,1)S(1)} %pad_maximum_fusion.refs_4_, ...), custom_call_target="tpu_custom_call" | custom-call | flops 1 | bytes 1 | tf_op jit(solution)/shard_map/attend/pallas_call | solution.py:419
  40.6 3.5 %collective-permute-done.8.above_ref.refs_6_ = bf16[256,512]{1,0:T(8,128)(2,1)S(1)} collective-permute-done((bf16[256,512]{1,0:T(8,128)(2,1)S(1)}, bf16[256,512]{1,0:T(8,128)(2,1)S(1)}, u32[]{:S(2)}, u32[]{:S(2)}) %collective-permute-start.8) | collective-permute-done | bytes 262176 | tf_op jit(solution)/shard_map/ppermute | solution.py:566
  44.1 1.4 %collective-permute-done.9.below_ref.refs_8_ = bf16[256,512]{1,0:T(8,128)(2,1)S(1)} collective-permute-done((bf16[256,512]{1,0:T(8,128)(2,1)S(1)}, bf16[256,512]{1,0:T(8,128)(2,1)S(1)}, u32[]{:S(2)}, u32[]{:S(2)}) %collective-permute-start.9) | collective-permute-done | bytes 262176 | tf_op jit(solution)/shard_map/ppermute | solution.py:566
  45.5 0.0 collective-permute-done.10.refs_5_.refs_7_
  45.6 1.6 %collective-permute-start.13 = (bf16[512,512]{1,0:T(8,128)(2,1)S(1)}, bf16[512,512]{1,0:T(8,128)(2,1)S(1)}, u32[]{:S(2)}, u32[]{:S(2)}) collective-permute-start(bf16[512,512]{1,0:T(8,128)(2,1)S(1)} %joined.5), channel_id=1, source_target_pairs={{4,0},{6,2},{0,4},{2,6},{12,8},{14,10},{8,12},{10,14},{20,16},{22,... | collective-permute-start | bytes 1572872 | tf_op jit(solution)/shard_map/ppermute | solution.py:572
  47.2 1.3 %collective-permute-start.11 = (bf16[512,512]{1,0:T(8,128)(2,1)S(1)}, bf16[512,512]{1,0:T(8,128)(2,1)S(1)}, u32[]{:S(2)}, u32[]{:S(2)}) collective-permute-start(bf16[512,512]{1,0:T(8,128)(2,1)S(1)} %joined.4), channel_id=1, source_target_pairs={{8,0},{10,2},{12,4},{14,6},{16,24},{18,26},{20,28},{22,30},{9,1},{... | collective-permute-start | bytes 1572872 | tf_op jit(solution)/shard_map/ppermute | solution.py:566
  48.5 0.7 collective-permute-start.12
  49.2 7.6 %attend.6.refs_4_ = f32[2,6,144,256]{3,2,1,0:T(8,128)S(1)} custom-call(s32[1]{0:T(128)} %bitcast.own_ref.refs_0_, s32[16]{0:T(128)S(1)} %copy-done.2, s32[8,8]{1,0:T(8,128)S(1)} %copy-done.1, bf16[2,6,256,256]{3,2,1,0:T(8,128)(2,1)S(1)} %turn.1.refs_3_, f32[2,6,144,256]{3,2,1,0:T(8,128)S(1)} %attend.5.refs_4_, ...), custom_call_target="tpu_custom_call" | custom-call | flops 1 | bytes 1 | tf_op jit(solution)/shard_map/attend/pallas_call | solution.py:419
  56.7 1.0 collective-permute-done.13.refs_6_.refs_8_.x_ref
  57.7 3.1 %collective-permute-done.11.ends_ref = bf16[512,512]{1,0:T(8,128)(2,1)S(1)} collective-permute-done((bf16[512,512]{1,0:T(8,128)(2,1)S(1)}, bf16[512,512]{1,0:T(8,128)(2,1)S(1)}, u32[]{:S(2)}, u32[]{:S(2)}) %collective-permute-start.11) | collective-permute-done | bytes 524320 | tf_op jit(solution)/shard_map/ppermute | solution.py:566
  60.9 0.0 collective-permute-done.12.middle_ref
  60.9 0.1 picked.1
  60.9 0.6 collective-permute-start.14
  61.5 4.7 %collective-permute-start.15 = (bf16[256,512]{1,0:T(8,128)(2,1)S(1)}, bf16[256,512]{1,0:T(8,128)(2,1)S(1)}, u32[]{:S(2)}, u32[]{:S(2)}) collective-permute-start(bf16[256,512]{1,0:T(8,128)(2,1)S(1)} %lower_half.1), channel_id=1, source_target_pairs={{0,8},{2,10},{4,12},{6,14},{8,0},{10,2},{12,4},{14,6},{16,24},{18,... | collective-permute-start | bytes 786440 | tf_op jit(solution)/shard_map/ppermute | solution.py:566
  66.2 8.1 %attend.7.refs_4_ = f32[2,6,144,256]{3,2,1,0:T(8,128)S(1)} custom-call(s32[1]{0:T(128)} %bitcast.own_ref.refs_0_, s32[16]{0:T(128)S(1)} %copy-done.2, s32[8,8]{1,0:T(8,128)S(1)} %copy-done.1, bf16[2,6,256,256]{3,2,1,0:T(8,128)(2,1)S(1)} %turn.1.refs_3_, f32[2,6,144,256]{3,2,1,0:T(8,128)S(1)} %attend.6.refs_4_, ...), custom_call_target="tpu_custom_call" | custom-call | flops 1 | bytes 1 | tf_op jit(solution)/shard_map/attend/pallas_call | solution.py:419
  74.3 0.0 collective-permute-done.14.refs_5_
  74.3 0.0 collective-permute-done.15.refs_6_
  74.3 3.5 %attend.8 = (bf16[128,768]{1,0:T(8,128)(2,1)S(1)}, bf16[128,768]{1,0:T(8,128)(2,1)S(1)}) custom-call(s32[1]{0:T(128)} %bitcast.own_ref.refs_0_, s32[16]{0:T(128)S(1)} %copy-done.2, s32[8,8]{1,0:T(8,128)S(1)} %copy-done.1, bf16[2,6,256,256]{3,2,1,0:T(8,128)(2,1)S(1)} %turn.1.refs_3_, f32[2,6,144,256]{3,2,1,0:T(8,128)S(1)} %attend.7.refs_4_, ...), custom_call_target="tpu_custom_call" | custom-call | flops 1 | bytes 1 | tf_op jit(solution)/shard_map/attend/pallas_call | solution.py:419
  77.9 0.1 collective-permute-start.16
  78.0 1.7 %project.3.refs_3_ = f32[128,3072]{1,0:T(8,128)S(1)} custom-call(s32[1]{0:T(128)} %bitcast.own_ref.refs_0_, bf16[128,768]{1,0:T(8,128)(2,1)S(1)} %get-tuple-element.59.refs_1_, bf16[1536,3072]{1,0:T(8,128)(2,1)S(1)} %fetch.1.refs_2_.refs_3_), custom_call_target="tpu_custom_call" | custom-call | flops 603979776 | bytes 4718592 | tf_op jit(solution)/shard_map/project/pallas_call | solution.py:525
  79.6 0.0 collective-permute-done.16.refs_1_
  79.7 1.7 %project.4 = bf16[128,3072]{1,0:T(8,128)(2,1)S(1)} custom-call(s32[1]{0:T(128)} %bitcast.own_ref.refs_0_, bf16[128,768]{1,0:T(8,128)(2,1)S(1)} %collective-permute-done.16.refs_1_, bf16[1536,3072]{1,0:T(8,128)(2,1)S(1)} %fetch.1.refs_2_.refs_3_, f32[128,3072]{1,0:T(8,128)S(1)} %project.3.refs_3_), custom_call_target="tpu_custom_call" | custom-call | flops 603979776 | bytes 4718592 | tf_op jit(solution)/shard_map/project/pallas_call | solution.py:525
  81.4 0.0 copy-start
  81.4 0.0 copy-start.3
  81.4 0.6 collective-permute-start.18
  82.0 3.3 %attend.9 = (bf16[128,768]{1,0:T(8,128)(2,1)S(1)}, bf16[128,768]{1,0:T(8,128)(2,1)S(1)}) custom-call(s32[1]{0:T(128)} %bitcast.own_ref.refs_0_, s32[16]{0:T(128)S(1)} %copy-done.2, s32[8,8]{1,0:T(8,128)S(1)} %copy-done.1, bf16[2,6,256,256]{3,2,1,0:T(8,128)(2,1)S(1)} %turn.1.refs_3_, f32[2,6,144,256]{3,2,1,0:T(8,128)S(1)} %attend.7.refs_4_, ...), custom_call_target="tpu_custom_call" | custom-call | flops 1 | bytes 1 | tf_op jit(solution)/shard_map/attend/pallas_call | solution.py:419
  85.3 0.3 collective-permute-start.17
  85.6 1.2 %collective-permute-done.17.refs_2_ = bf16[128,768]{1,0:T(8,128)(2,1)S(1)} collective-permute-done((bf16[128,768]{1,0:T(8,128)(2,1)S(1)}, bf16[128,768]{1,0:T(8,128)(2,1)S(1)}, u32[]{:S(2)}, u32[]{:S(2)}) %collective-permute-start.17) | collective-permute-done | bytes 196640 | tf_op jit(solution)/shard_map/ppermute | solution.py:560
  86.8 0.0 copy-done
  86.9 0.0 copy-done.3
  86.9 3.9 %project.5 = (f32[128,3072]{1,0:T(8,128)S(1)}, f32[8,3072]{1,0:T(8,128)S(1)}) custom-call(s32[1]{0:T(128)} %bitcast.own_ref.refs_0_, bf16[128,768]{1,0:T(8,128)(2,1)S(1)} %get-tuple-element.61.refs_1_, bf16[128,768]{1,0:T(8,128)(2,1)S(1)} %collective-permute-done.17.refs_2_, bf16[1536,3072]{1,0:T(8,128)(2,1)S(1)} %fetch.1.refs_2_.refs_3_, s32[8]{0:T(128)S(1)} %copy-done.3, ...), custom_call_target="tpu_custom_call" | custom-call | flops 1207959552 | bytes 9437184 | tf_op jit(solution)/shard_map/project/pallas_call | solution.py:525
  90.8 10.6 %collective-permute-done.18 = bf16[128,3072]{1,0:T(8,128)(2,1)S(1)} collective-permute-done((bf16[128,3072]{1,0:T(8,128)(2,1)S(1)}, bf16[128,3072]{1,0:T(8,128)(2,1)S(1)}, u32[]{:S(2)}, u32[]{:S(2)}) %collective-permute-start.18) | collective-permute-done | bytes 786464 | tf_op jit(solution)/shard_map/ppermute | solution.py:636
  101.4 1.1 %add_convert_fusion = bf16[128,3072]{1,0:T(8,128)(2,1)} fusion(f32[128,3072]{1,0:T(8,128)S(1)} %get-tuple-element.63, bf16[128,3072]{1,0:T(8,128)(2,1)S(1)} %collective-permute-done.18, f32[3072]{0:T(1024)S(1)} %bitcast.2), kind=kLoop, calls=%fused_computation | loop fusion | flops 1572864 | bytes 3158016 | tf_op jit(solution)/shard_map/convert_element_type | solution.py:641
  (12 shorter events, 0.3 us)
Async XLA Ops:
  0.0 4.5 %copy-start.4 = (bf16[128,3072]{1,0:T(8,128)(2,1)S(1)}, bf16[128,3072]{1,0:T(8,128)(2,1)}, u32[]{:S(2)}) copy-start(bf16[128,3072]{1,0:T(8,128)(2,1)} %param.9) | copy-start | bytes 2359300
  1.2 6.9 %collective-permute-start.1 = (bf16[128,512]{1,0:T(8,128)(2,1)S(1)}, bf16[128,512]{1,0:T(8,128)(2,1)S(1)}, u32[]{:S(2)}, u32[]{:S(2)}) collective-permute-start(bf16[128,512]{1,0:T(8,128)(2,1)S(1)} %pad_maximum_fusion.4), channel_id=1, source_target_pairs={{1,0},{0,1},{3,2},{2,3},{5,4},{4,5},{7,6},{6,7},{9,8},{8,9},{11,10... | collective-permute-start | bytes 393224 | tf_op jit(solution)/shard_map/ppermute | solution.py:560
  4.2 5.9 %collective-permute-start.2 = (bf16[128,512]{1,0:T(8,128)(2,1)S(1)}, bf16[128,512]{1,0:T(8,128)(2,1)S(1)}, u32[]{:S(2)}, u32[]{:S(2)}) collective-permute-start(bf16[128,512]{1,0:T(8,128)(2,1)S(1)} %pad_maximum_fusion.5), channel_id=1, source_target_pairs={{3,0},{2,1},{1,2},{0,3},{7,4},{6,5},{5,6},{4,7},{11,8},{10,9},{9,1... | collective-permute-start | bytes 393224 | tf_op jit(solution)/shard_map/ppermute | solution.py:560
  4.3 5.9 %collective-permute-start = (bf16[128,512]{1,0:T(8,128)(2,1)S(1)}, bf16[128,512]{1,0:T(8,128)(2,1)S(1)}, u32[]{:S(2)}, u32[]{:S(2)}) collective-permute-start(bf16[128,512]{1,0:T(8,128)(2,1)S(1)} %pad_maximum_fusion.3), channel_id=1, source_target_pairs={{2,0},{3,1},{0,2},{1,3},{6,4},{7,5},{4,6},{5,7},{10,8},{11,9},{8,1... | collective-permute-start | bytes 393224 | tf_op jit(solution)/shard_map/ppermute | solution.py:560
  10.2 19.0 %collective-permute-start.3 = (bf16[512,512]{1,0:T(8,128)(2,1)S(1)}, bf16[512,512]{1,0:T(8,128)(2,1)S(1)}, u32[]{:S(2)}, u32[]{:S(2)}) collective-permute-start(bf16[512,512]{1,0:T(8,128)(2,1)S(1)} %pad_maximum_fusion.refs_4_), channel_id=1, source_target_pairs={{4,0},{6,2},{0,4},{2,6},{12,8},{14,10},{8,12},{10,14},{20,16},{22,... | collective-permute-start | bytes 1572872 | tf_op jit(solution)/shard_map/ppermute | solution.py:572
  11.8 17.5 %collective-permute-start.6 = (bf16[128,1536]{1,0:T(8,128)(2,1)S(1)}, bf16[128,1536]{1,0:T(8,128)(2,1)S(1)}, u32[]{:S(2)}, u32[]{:S(2)}) collective-permute-start(bf16[128,1536]{1,0:T(8,128)(2,1)S(1)} %get-tuple-element.39), channel_id=1, source_target_pairs={{1,0},{0,1},{3,2},{2,3},{5,4},{4,5},{7,6},{6,7},{9,8},{8,9},{11,10... | collective-permute-start | bytes 1179656 | tf_op jit(solution)/shard_map/ppermute | solution.py:560
  12.8 14.1 %collective-permute-start.4 = (bf16[256,512]{1,0:T(8,128)(2,1)S(1)}, bf16[256,512]{1,0:T(8,128)(2,1)S(1)}, u32[]{:S(2)}, u32[]{:S(2)}) collective-permute-start(bf16[256,512]{1,0:T(8,128)(2,1)S(1)} %pad_maximum_fusion.1), channel_id=1, source_target_pairs={{0,8},{2,10},{4,12},{6,14},{8,0},{10,2},{12,4},{14,6},{16,24},{18,... | collective-permute-start | bytes 786440 | tf_op jit(solution)/shard_map/ppermute | solution.py:566
  14.4 14.9 %collective-permute-start.5 = (bf16[256,512]{1,0:T(8,128)(2,1)S(1)}, bf16[256,512]{1,0:T(8,128)(2,1)S(1)}, u32[]{:S(2)}, u32[]{:S(2)}) collective-permute-start(bf16[256,512]{1,0:T(8,128)(2,1)S(1)} %pad_maximum_fusion.1), channel_id=1, source_target_pairs={{0,16},{2,18},{4,20},{6,22},{8,24},{10,26},{12,28},{14,30},{16,0},... | collective-permute-start | bytes 786440 | tf_op jit(solution)/shard_map/ppermute | solution.py:566
  29.3 16.2 %collective-permute-start.10 = (bf16[512,512]{1,0:T(8,128)(2,1)S(1)}, bf16[512,512]{1,0:T(8,128)(2,1)S(1)}, u32[]{:S(2)}, u32[]{:S(2)}) collective-permute-start(bf16[512,512]{1,0:T(8,128)(2,1)S(1)} %joined.3), channel_id=1, source_target_pairs={{4,0},{6,2},{0,4},{2,6},{12,8},{14,10},{8,12},{10,14},{20,16},{22,... | collective-permute-start | bytes 1572872 | tf_op jit(solution)/shard_map/ppermute | solution.py:572
  29.9 3.6 %copy-start.1 = (s32[8,8]{1,0:T(8,128)S(1)}, s32[8,8]{1,0:T(8,128)}, u32[]{:S(2)}) copy-start(s32[8,8]{1,0:T(8,128)} %refs_2_.9) | copy-start | bytes 772
  29.9 3.6 %copy-start.2 = (s32[16]{0:T(128)S(1)}, s32[16]{0:T(128)}, u32[]{:S(2)}) copy-start(s32[16]{0:T(128)} %refs_5_.1) | copy-start | bytes 196
  30.0 3.2 %collective-permute-start.7 = (bf16[256,768]{1,0:T(8,128)(2,1)S(1)}, bf16[256,768]{1,0:T(8,128)(2,1)S(1)}, u32[]{:S(2)}, u32[]{:S(2)}) collective-permute-start(bf16[256,768]{1,0:T(8,128)(2,1)S(1)} %other_columns.1), channel_id=1, source_target_pairs={{2,0},{3,1},{0,2},{1,3},{6,4},{7,5},{4,6},{5,7},{10,8},{11,9},{8,1... | collective-permute-start | bytes 1179656 | tf_op jit(solution)/shard_map/ppermute | solution.py:560
  30.0 14.0 %collective-permute-start.8 = (bf16[256,512]{1,0:T(8,128)(2,1)S(1)}, bf16[256,512]{1,0:T(8,128)(2,1)S(1)}, u32[]{:S(2)}, u32[]{:S(2)}) collective-permute-start(bf16[256,512]{1,0:T(8,128)(2,1)S(1)} %pad_maximum_fusion.2), channel_id=1, source_target_pairs={{0,8},{2,10},{4,12},{6,14},{8,0},{10,2},{12,4},{14,6},{16,24},{18,... | collective-permute-start | bytes 786440 | tf_op jit(solution)/shard_map/ppermute | solution.py:566
  30.6 14.9 %collective-permute-start.9 = (bf16[256,512]{1,0:T(8,128)(2,1)S(1)}, bf16[256,512]{1,0:T(8,128)(2,1)S(1)}, u32[]{:S(2)}, u32[]{:S(2)}) collective-permute-start(bf16[256,512]{1,0:T(8,128)(2,1)S(1)} %pad_maximum_fusion.2), channel_id=1, source_target_pairs={{0,16},{2,18},{4,20},{6,22},{8,24},{10,26},{12,28},{14,30},{16,0},... | collective-permute-start | bytes 786440 | tf_op jit(solution)/shard_map/ppermute | solution.py:566
  45.6 12.1 %collective-permute-start.13 = (bf16[512,512]{1,0:T(8,128)(2,1)S(1)}, bf16[512,512]{1,0:T(8,128)(2,1)S(1)}, u32[]{:S(2)}, u32[]{:S(2)}) collective-permute-start(bf16[512,512]{1,0:T(8,128)(2,1)S(1)} %joined.5), channel_id=1, source_target_pairs={{4,0},{6,2},{0,4},{2,6},{12,8},{14,10},{8,12},{10,14},{20,16},{22,... | collective-permute-start | bytes 1572872 | tf_op jit(solution)/shard_map/ppermute | solution.py:572
  47.2 13.7 %collective-permute-start.11 = (bf16[512,512]{1,0:T(8,128)(2,1)S(1)}, bf16[512,512]{1,0:T(8,128)(2,1)S(1)}, u32[]{:S(2)}, u32[]{:S(2)}) collective-permute-start(bf16[512,512]{1,0:T(8,128)(2,1)S(1)} %joined.4), channel_id=1, source_target_pairs={{8,0},{10,2},{12,4},{14,6},{16,24},{18,26},{20,28},{22,30},{9,1},{... | collective-permute-start | bytes 1572872 | tf_op jit(solution)/shard_map/ppermute | solution.py:566
  48.5 12.4 %collective-permute-start.12 = (bf16[512,512]{1,0:T(8,128)(2,1)S(1)}, bf16[512,512]{1,0:T(8,128)(2,1)S(1)}, u32[]{:S(2)}, u32[]{:S(2)}) collective-permute-start(bf16[512,512]{1,0:T(8,128)(2,1)S(1)} %pad_maximum_fusion.refs_4_), channel_id=1, source_target_pairs={{8,16},{10,18},{12,20},{14,22},{16,8},{18,10},{20,12},{22,14},{9,1... | collective-permute-start | bytes 1572872 | tf_op jit(solution)/shard_map/ppermute | solution.py:566
  60.9 13.4 %collective-permute-start.14 = (bf16[256,512]{1,0:T(8,128)(2,1)S(1)}, bf16[256,512]{1,0:T(8,128)(2,1)S(1)}, u32[]{:S(2)}, u32[]{:S(2)}) collective-permute-start(bf16[256,512]{1,0:T(8,128)(2,1)S(1)} %get-tuple-element.56), channel_id=1, source_target_pairs={{4,0},{6,2},{0,4},{2,6},{12,8},{14,10},{8,12},{10,14},{20,16},{22,... | collective-permute-start | bytes 786440 | tf_op jit(solution)/shard_map/ppermute | solution.py:572
  61.5 12.8 %collective-permute-start.15 = (bf16[256,512]{1,0:T(8,128)(2,1)S(1)}, bf16[256,512]{1,0:T(8,128)(2,1)S(1)}, u32[]{:S(2)}, u32[]{:S(2)}) collective-permute-start(bf16[256,512]{1,0:T(8,128)(2,1)S(1)} %lower_half.1), channel_id=1, source_target_pairs={{0,8},{2,10},{4,12},{6,14},{8,0},{10,2},{12,4},{14,6},{16,24},{18,... | collective-permute-start | bytes 786440 | tf_op jit(solution)/shard_map/ppermute | solution.py:566
  77.9 1.8 %collective-permute-start.16 = (bf16[128,768]{1,0:T(8,128)(2,1)S(1)}, bf16[128,768]{1,0:T(8,128)(2,1)S(1)}, u32[]{:S(2)}, u32[]{:S(2)}) collective-permute-start(bf16[128,768]{1,0:T(8,128)(2,1)S(1)} %get-tuple-element.57), channel_id=1, source_target_pairs={{2,0},{3,1},{0,2},{1,3},{6,4},{7,5},{4,6},{5,7},{10,8},{11,9},{8,1... | collective-permute-start | bytes 589832 | tf_op jit(solution)/shard_map/ppermute | solution.py:560
  81.4 5.5 %copy-start = (bf16[128,3072]{1,0:T(8,128)(2,1)S(1)}, bf16[128,3072]{1,0:T(8,128)(2,1)}, u32[]{:S(2)}) copy-start(bf16[128,3072]{1,0:T(8,128)(2,1)} %refs_7_.1) | copy-start | bytes 2359300
  81.4 5.5 %copy-start.3 = (s32[8]{0:T(128)S(1)}, s32[8]{0:T(128)}, u32[]{:S(2)}) copy-start(s32[8]{0:T(128)} %refs_4_.1) | copy-start | bytes 100
  81.4 20.0 %collective-permute-start.18 = (bf16[128,3072]{1,0:T(8,128)(2,1)S(1)}, bf16[128,3072]{1,0:T(8,128)(2,1)S(1)}, u32[]{:S(2)}, u32[]{:S(2)}) collective-permute-start(bf16[128,3072]{1,0:T(8,128)(2,1)S(1)} %project.4), channel_id=1, source_target_pairs={{0,1},{1,0},{2,3},{3,2},{4,5},{5,4},{6,7},{7,6},{8,9},{9,8},{10,11... | collective-permute-start | bytes 2359304 | tf_op jit(solution)/shard_map/ppermute | solution.py:636
  85.3 1.5 %collective-permute-start.17 = (bf16[128,768]{1,0:T(8,128)(2,1)S(1)}, bf16[128,768]{1,0:T(8,128)(2,1)S(1)}, u32[]{:S(2)}, u32[]{:S(2)}) collective-permute-start(bf16[128,768]{1,0:T(8,128)(2,1)S(1)} %get-tuple-element.62), channel_id=1, source_target_pairs={{2,0},{3,1},{0,2},{1,3},{6,4},{7,5},{4,6},{5,7},{10,8},{11,9},{8,1... | collective-permute-start | bytes 589832 | tf_op jit(solution)/shard_map/ppermute | solution.py:560
